TPU v7x, 32 devices: a whole 2x2x4 slice. The times are simulated.
32 devices in a mesh: dp: 4 (over y, core), fsdp: 8 (over z, x).
Axes of the slice: x: 2, y: 2, z: 4, core: 2. Of those that a mesh axis runs over, the one named last changes fastest.
Arguments:
- tokens: bfloat16 [8192, 768], P(('dp', 'fsdp')), may hold values from -6 to 6
- segment_ids: int32 [32, 256], P(('dp', 'fsdp')), may hold values from 0 to 3, never falling along the last dimension, each value on 1 to 128 neighbouring positions
- neighbours: bfloat16 [256, 128, 768], P(('dp', 'fsdp')), may hold values from -6 to 6
- neighbour_ids: int32 [32, 4, 2], P(('dp', 'fsdp')), may hold values from 0 to 255, as said below
- neighbour_tokens: int32 [256, 128], P(('dp', 'fsdp')), may hold values from 0 to 50256, as said below
- gains_one: bfloat16 [3, 768], P(None, ('dp', 'fsdp')), may hold values from 0.5 to 1.5
- biases_one: bfloat16 [10, 768], P(None, ('dp', 'fsdp')), may hold values from -1 to 1
- w_qkv_one: bfloat16 [768, 2304], P(('dp', 'fsdp')), may hold values from -0.21875 to 0.21875
- w_out_one: bfloat16 [768, 768], P(('dp', 'fsdp')), may hold values from -0.625 to 0.625
- w_cross_q: bfloat16 [768, 768], P(('dp', 'fsdp')), may hold values from -0.21875 to 0.21875
- w_cross_kv: bfloat16 [768, 1536], P(('dp', 'fsdp')), may hold values from -0.21875 to 0.21875
- w_cross_out: bfloat16 [768, 768], P(('dp', 'fsdp')), may hold values from -0.625 to 0.625
- w_up_one: bfloat16 [768, 3072], P(('dp', 'fsdp')), may hold values from -0.21875 to 0.21875
- bias_up_one: bfloat16 [3072], P(('dp', 'fsdp')), may hold values from -1 to 1
- w_down_one: bfloat16 [3072, 768], P(('dp', 'fsdp')), may hold values from -0.109375 to 0.109375
- gains_two: bfloat16 [2, 768], P(None, ('dp', 'fsdp')), may hold values from 0.5 to 1.5
- biases_two: bfloat16 [6, 768], P(None, ('dp', 'fsdp')), may hold values from -1 to 1
- w_qkv_two: bfloat16 [768, 2304], P(('dp', 'fsdp')), may hold values from -0.21875 to 0.21875
- w_out_two: bfloat16 [768, 768], P(('dp', 'fsdp')), may hold values from -0.625 to 0.625
- w_up_two: bfloat16 [768, 3072], P(('dp', 'fsdp')), may hold values from -0.21875 to 0.21875
- bias_up_two: bfloat16 [3072], P(('dp', 'fsdp')), may hold values from -1 to 1
- w_down_two: bfloat16 [3072, 768], P(('dp', 'fsdp')), may hold values from -0.109375 to 0.109375
- cotangent: bfloat16 [8192, 768], P(('dp', 'fsdp')), may hold values from -6 to 6
Outputs:
- out: bfloat16 [8192, 768], P(('dp', 'fsdp'))
- grad_tokens: float32 [8192, 768], P(('dp', 'fsdp'))
- grad_neighbours: float32 [256, 128, 768], P(('dp', 'fsdp'))
- grad_gains_one: float32 [3, 768], P(None, ('dp', 'fsdp'))
- grad_biases_one: float32 [10, 768], P(None, ('dp', 'fsdp'))
- grad_w_qkv_one: float32 [768, 2304], P(('dp', 'fsdp'))
- grad_w_out_one: float32 [768, 768], P(('dp', 'fsdp'))
- grad_w_cross_q: float32 [768, 768], P(('dp', 'fsdp'))
- grad_w_cross_kv: float32 [768, 1536], P(('dp', 'fsdp'))
- grad_w_cross_out: float32 [768, 768], P(('dp', 'fsdp'))
- grad_w_up_one: float32 [768, 3072], P(('dp', 'fsdp'))
- grad_bias_up_one: float32 [3072], P(('dp', 'fsdp'))
- grad_w_down_one: float32 [3072, 768], P(('dp', 'fsdp'))
- grad_gains_two: float32 [2, 768], P(None, ('dp', 'fsdp'))
- grad_biases_two: float32 [6, 768], P(None, ('dp', 'fsdp'))
- grad_w_qkv_two: float32 [768, 2304], P(('dp', 'fsdp'))
- grad_w_out_two: float32 [768, 768], P(('dp', 'fsdp'))
- grad_w_up_two: float32 [768, 3072], P(('dp', 'fsdp'))
- grad_bias_up_two: float32 [3072], P(('dp', 'fsdp'))
- grad_w_down_two: float32 [3072, 768], P(('dp', 'fsdp'))
Inputs may be any that keep to these rules, and one draw needn't show every extreme that they name: `segment_ids`: within each row the ids never fall. `neighbour_ids`: the spans of sequence s name, each once, the 8 neighbours stored with that sequence, numbers s * 2 * 4 onward. `neighbour_tokens`: in each neighbour the nonzero ids come first, a quarter of 128 of them or more; zeros after them are padding.
All inputs are finite; a program needn't handle non-finite values.
Results may differ from a plain program's by a relative error of at most 0.023.
Values may be sent and summed in bfloat16 or wider, within the bound.
A program may use at most 256 MiB of HBM per device.

v0:
```python
import jax
import jax.numpy as jnp
from jax import lax
from jax.sharding import PartitionSpec as P

HEADS = 12
HEAD_DIM = 64


def layer_norm(hidden, norm_gain, norm_bias):
    centred = hidden - jnp.mean(hidden, axis=-1, keepdims=True)
    spread = jnp.mean(centred * centred, axis=-1, keepdims=True)
    return centred * lax.rsqrt(spread + 1e-05) * norm_gain + norm_bias


def norm_backward(hidden, norm_gain, norm_bias, gradient):
    _, pullback = jax.vjp(layer_norm, hidden, norm_gain, norm_bias)
    return pullback(gradient)


def gelu_tanh(values):
    return jax.nn.gelu(values, approximate=True)


def product(left, right):
    return jnp.dot(left, right, preferred_element_type=jnp.float32)


def column_sums(values):
    return jnp.sum(values.astype(jnp.float32), axis=0)


def flat_rows(values):
    return values.reshape(-1, 128)


def restore_rows(values, width):
    return values.reshape(-1, width)


def softmax_rows(scores):
    row_top = jnp.max(scores, axis=-1, keepdims=True)
    shifted = jnp.exp(scores - row_top)
    row_total = jnp.sum(shifted, axis=-1, keepdims=True)
    return (shifted / row_total, row_top + jnp.log(row_total))


def self_scores(packed, allowed):
    scores = jnp.einsum(
        "qhe,khe->hqk", packed[:, 0], packed[:, 1], preferred_element_type=jnp.float32
    ) * HEAD_DIM ** (-0.5)
    return jnp.where(allowed[None], scores, -1e30)


def self_forward(normed, w_packed, bias_query, bias_value, w_output, bias_output, allowed):
    row_count, model_width = normed.shape
    packed_bias = jnp.concatenate([bias_query, jnp.zeros_like(bias_query), bias_value]).astype(
        jnp.float32
    )
    packed = (
        (product(normed, w_packed) + packed_bias)
        .astype(jnp.bfloat16)
        .reshape(row_count, 3, HEADS, HEAD_DIM)
    )
    attn_probs, logsum = softmax_rows(self_scores(packed, allowed))
    mixed_heads = jnp.einsum(
        "hqk,khe->qhe",
        attn_probs.astype(jnp.bfloat16),
        packed[:, 2],
        preferred_element_type=jnp.float32,
    )
    mixed_heads = mixed_heads.astype(jnp.bfloat16).reshape(row_count, model_width)
    branch = product(mixed_heads, w_output) + bias_output.astype(jnp.float32)
    return (branch, (packed, logsum, mixed_heads))


def self_backward(normed, w_packed, w_output, allowed, kept_values, gradient):
    packed, logsum, mixed_heads = kept_values
    row_count, model_width = normed.shape
    score_scale = HEAD_DIM ** (-0.5)
    grad_low = gradient.astype(jnp.bfloat16)
    grad_bias_output = column_sums(grad_low)
    grad_w_output = product(mixed_heads.T, grad_low)
    grad_mixed = (
        product(grad_low, w_output.T).astype(jnp.bfloat16).reshape(row_count, HEADS, HEAD_DIM)
    )
    attn_probs = jnp.exp(self_scores(packed, allowed) - logsum)
    grad_probs = jnp.einsum(
        "qhe,khe->hqk", grad_mixed, packed[:, 2], preferred_element_type=jnp.float32
    )
    grad_values = jnp.einsum(
        "hqk,qhe->khe",
        attn_probs.astype(jnp.bfloat16),
        grad_mixed,
        preferred_element_type=jnp.float32,
    )
    grad_scores = attn_probs * (
        grad_probs - jnp.sum(attn_probs * grad_probs, axis=-1, keepdims=True)
    )
    grad_scores = grad_scores.astype(jnp.bfloat16)
    grad_queries = (
        jnp.einsum("hqk,khe->qhe", grad_scores, packed[:, 1], preferred_element_type=jnp.float32)
        * score_scale
    )
    grad_keys = (
        jnp.einsum("hqk,qhe->khe", grad_scores, packed[:, 0], preferred_element_type=jnp.float32)
        * score_scale
    )
    grad_packed = (
        jnp.stack([grad_queries, grad_keys, grad_values], axis=1)
        .astype(jnp.bfloat16)
        .reshape(row_count, 3 * model_width)
    )
    grad_packed_bias = column_sums(grad_packed)
    grad_w_packed = product(normed.T, grad_packed)
    grad_normed = product(grad_packed, w_packed.T)
    return (
        grad_normed,
        grad_w_packed,
        grad_w_output,
        grad_packed_bias[:model_width],
        grad_packed_bias[2 * model_width :],
        grad_bias_output,
    )


def cross_scores(queries, key_value, near_valid):
    scores = jnp.einsum(
        "cqhe,ckhe->chqk", queries, key_value[:, :, 0], preferred_element_type=jnp.float32
    ) * HEAD_DIM ** (-0.5)
    return jnp.where(near_valid[:, None, None, :], scores, -1e30)


def cross_forward(
    normed, near_rows, near_valid, w_query, bias_query, w_pair, bias_value, w_output, bias_output
):
    row_count, model_width = normed.shape
    span_count, key_count = (near_rows.shape[0], near_rows.shape[1])
    queries = (product(normed, w_query) + bias_query.astype(jnp.float32)).astype(jnp.bfloat16)
    queries = queries.reshape(span_count, row_count // span_count, HEADS, HEAD_DIM)
    pair_bias = jnp.concatenate([jnp.zeros_like(bias_value), bias_value]).astype(jnp.float32)
    key_value = product(near_rows.reshape(span_count * key_count, model_width), w_pair) + pair_bias
    key_value = key_value.astype(jnp.bfloat16).reshape(span_count, key_count, 2, HEADS, HEAD_DIM)
    attn_probs, logsum = softmax_rows(cross_scores(queries, key_value, near_valid))
    mixed_heads = jnp.einsum(
        "chqk,ckhe->cqhe",
        attn_probs.astype(jnp.bfloat16),
        key_value[:, :, 1],
        preferred_element_type=jnp.float32,
    )
    mixed_heads = mixed_heads.astype(jnp.bfloat16).reshape(row_count, model_width)
    branch = product(mixed_heads, w_output) + bias_output.astype(jnp.float32)
    return (branch, (queries, key_value, logsum, mixed_heads))


def cross_backward(normed, near_rows, near_valid, w_query, w_pair, w_output, kept_values, gradient):
    queries, key_value, logsum, mixed_heads = kept_values
    row_count, model_width = normed.shape
    span_count, key_count = (near_rows.shape[0], near_rows.shape[1])
    score_scale = HEAD_DIM ** (-0.5)
    grad_low = gradient.astype(jnp.bfloat16)
    grad_bias_output = column_sums(grad_low)
    grad_w_output = product(mixed_heads.T, grad_low)
    grad_mixed = product(grad_low, w_output.T).astype(jnp.bfloat16)
    grad_mixed = grad_mixed.reshape(span_count, row_count // span_count, HEADS, HEAD_DIM)
    attn_probs = jnp.exp(cross_scores(queries, key_value, near_valid) - logsum)
    grad_probs = jnp.einsum(
        "cqhe,ckhe->chqk", grad_mixed, key_value[:, :, 1], preferred_element_type=jnp.float32
    )
    grad_values = jnp.einsum(
        "chqk,cqhe->ckhe",
        attn_probs.astype(jnp.bfloat16),
        grad_mixed,
        preferred_element_type=jnp.float32,
    )
    grad_scores = attn_probs * (
        grad_probs - jnp.sum(attn_probs * grad_probs, axis=-1, keepdims=True)
    )
    grad_scores = grad_scores.astype(jnp.bfloat16)
    grad_queries = (
        jnp.einsum(
            "chqk,ckhe->cqhe", grad_scores, key_value[:, :, 0], preferred_element_type=jnp.float32
        )
        * score_scale
    )
    grad_queries = grad_queries.astype(jnp.bfloat16).reshape(row_count, model_width)
    grad_keys = (
        jnp.einsum("chqk,cqhe->ckhe", grad_scores, queries, preferred_element_type=jnp.float32)
        * score_scale
    )
    grad_pair = (
        jnp.stack([grad_keys, grad_values], axis=2)
        .astype(jnp.bfloat16)
        .reshape(span_count * key_count, 2 * model_width)
    )
    grad_bias_query = column_sums(grad_queries)
    grad_w_query = product(normed.T, grad_queries)
    grad_normed = product(grad_queries, w_query.T)
    grad_bias_value = column_sums(grad_pair[:, model_width:])
    flat_near = near_rows.reshape(span_count * key_count, model_width)
    grad_w_pair = product(flat_near.T, grad_pair)
    grad_near = product(grad_pair, w_pair.T)
    return (
        grad_normed,
        grad_near,
        grad_w_query,
        grad_w_pair,
        grad_w_output,
        grad_bias_query,
        grad_bias_value,
        grad_bias_output,
    )


def mlp_forward(normed, w_up, bias_up, w_down, bias_down):
    hidden = product(normed, w_up) + bias_up.astype(jnp.float32)
    active = gelu_tanh(hidden).astype(jnp.bfloat16)
    return (product(active, w_down) + bias_down.astype(jnp.float32), (hidden, active))


def mlp_backward(normed, w_up, w_down, kept_values, gradient):
    hidden, active = kept_values
    grad_low = gradient.astype(jnp.bfloat16)
    grad_bias_down = column_sums(grad_low)
    grad_w_down = product(active.T, grad_low)
    grad_active = product(grad_low, w_down.T)
    _, pullback = jax.vjp(gelu_tanh, hidden)
    grad_hidden = pullback(grad_active)[0].astype(jnp.bfloat16)
    grad_bias_up = column_sums(grad_hidden)
    grad_w_up = product(normed.T, grad_hidden)
    grad_normed = product(grad_hidden, w_up.T)
    return (grad_normed, grad_w_up, grad_bias_up, grad_w_down, grad_bias_down)


def local(
    tokens,
    segment_ids,
    neighbours,
    neighbour_ids,
    neighbour_tokens,
    gains_one,
    biases_one,
    w_qkv_one,
    w_out_one,
    w_cross_q,
    w_cross_kv,
    w_cross_out,
    w_up_one,
    bias_up_one,
    w_down_one,
    gains_two,
    biases_two,
    w_qkv_two,
    w_out_two,
    w_up_two,
    bias_up_two,
    w_down_two,
    cotangent,
):
    row_count, model_width = tokens.shape
    hidden_width = w_up_one.shape[1]
    store_count, near_length = (neighbours.shape[0], neighbours.shape[1])
    span_count, near_count = (neighbour_ids.shape[1], neighbour_ids.shape[2])
    position = jnp.arange(row_count)
    segments = segment_ids[0]
    allowed = (position[:, None] >= position[None, :]) & (segments[:, None] == segments[None, :])
    near_index = neighbour_ids[0].reshape(-1) % store_count
    near_rows = jnp.take(neighbours, near_index, axis=0).reshape(
        span_count, near_count * near_length, model_width
    )
    near_valid = (jnp.take(neighbour_tokens, near_index, axis=0) != 0).reshape(
        span_count, near_count * near_length
    )
    whole_one = (
        lax.all_gather(gains_one, ("dp", "fsdp"), axis=1, tiled=True),
        lax.all_gather(biases_one, ("dp", "fsdp"), axis=1, tiled=True),
        lax.all_gather(w_qkv_one, ("dp", "fsdp"), axis=0, tiled=True),
        lax.all_gather(w_out_one, ("dp", "fsdp"), axis=0, tiled=True),
        lax.all_gather(w_cross_q, ("dp", "fsdp"), axis=0, tiled=True),
        lax.all_gather(w_cross_kv, ("dp", "fsdp"), axis=0, tiled=True),
        lax.all_gather(w_cross_out, ("dp", "fsdp"), axis=0, tiled=True),
        lax.all_gather(w_up_one, ("dp", "fsdp"), axis=0, tiled=True),
        lax.all_gather(bias_up_one, ("dp", "fsdp"), axis=0, tiled=True),
        lax.all_gather(w_down_one, ("dp", "fsdp"), axis=0, tiled=True),
    )
    (
        gains_a,
        biases_a,
        w_qkv_a,
        w_out_a,
        w_query_c,
        w_pair_c,
        w_out_c,
        w_up_a,
        bias_up_a,
        w_down_a,
    ) = whole_one
    gain_a = gains_a.astype(jnp.float32)
    shift_a = biases_a.astype(jnp.float32)
    state_zero = tokens.astype(jnp.float32)
    normed_first = layer_norm(state_zero, gain_a[0], shift_a[0]).astype(jnp.bfloat16)
    branch, kept_self_a = self_forward(
        normed_first, w_qkv_a, biases_a[3], biases_a[4], w_out_a, biases_a[5], allowed
    )
    state_one = state_zero + branch
    normed_second = layer_norm(state_one, gain_a[1], shift_a[1]).astype(jnp.bfloat16)
    branch, kept_cross = cross_forward(
        normed_second,
        near_rows,
        near_valid,
        w_query_c,
        biases_a[6],
        w_pair_c,
        biases_a[7],
        w_out_c,
        biases_a[8],
    )
    state_two = state_one + branch
    normed_third = layer_norm(state_two, gain_a[2], shift_a[2]).astype(jnp.bfloat16)
    branch, kept_mlp_a = mlp_forward(normed_third, w_up_a, bias_up_a, w_down_a, biases_a[9])
    state_three = state_two + branch
    whole_two = (
        lax.all_gather(gains_two, ("dp", "fsdp"), axis=1, tiled=True),
        lax.all_gather(biases_two, ("dp", "fsdp"), axis=1, tiled=True),
        lax.all_gather(w_qkv_two, ("dp", "fsdp"), axis=0, tiled=True),
        lax.all_gather(w_out_two, ("dp", "fsdp"), axis=0, tiled=True),
        lax.all_gather(w_up_two, ("dp", "fsdp"), axis=0, tiled=True),
        lax.all_gather(bias_up_two, ("dp", "fsdp"), axis=0, tiled=True),
        lax.all_gather(w_down_two, ("dp", "fsdp"), axis=0, tiled=True),
    )
    gains_b, biases_b, w_qkv_b, w_out_b, w_up_b, bias_up_b, w_down_b = whole_two
    gain_b = gains_b.astype(jnp.float32)
    shift_b = biases_b.astype(jnp.float32)
    normed_fourth = layer_norm(state_three, gain_b[0], shift_b[0]).astype(jnp.bfloat16)
    branch, kept_self_b = self_forward(
        normed_fourth, w_qkv_b, biases_b[2], biases_b[3], w_out_b, biases_b[4], allowed
    )
    state_four = state_three + branch
    normed_fifth = layer_norm(state_four, gain_b[1], shift_b[1]).astype(jnp.bfloat16)
    branch, kept_mlp_b = mlp_forward(normed_fifth, w_up_b, bias_up_b, w_down_b, biases_b[5])
    state_five = state_four + branch
    again_two = (
        lax.all_gather(gains_two, ("dp", "fsdp"), axis=1, tiled=True),
        lax.all_gather(biases_two, ("dp", "fsdp"), axis=1, tiled=True),
        lax.all_gather(w_qkv_two, ("dp", "fsdp"), axis=0, tiled=True),
        lax.all_gather(w_out_two, ("dp", "fsdp"), axis=0, tiled=True),
        lax.all_gather(w_up_two, ("dp", "fsdp"), axis=0, tiled=True),
        lax.all_gather(bias_up_two, ("dp", "fsdp"), axis=0, tiled=True),
        lax.all_gather(w_down_two, ("dp", "fsdp"), axis=0, tiled=True),
    )
    gains_b, biases_b, w_qkv_b, w_out_b, w_up_b, bias_up_b, w_down_b = again_two
    gain_b = gains_b.astype(jnp.float32)
    shift_b = biases_b.astype(jnp.float32)
    gradient = cotangent.astype(jnp.float32)
    grad_normed, grad_w_up_b, grad_bias_up_b, grad_w_down_b, grad_down_b = mlp_backward(
        normed_fifth, w_up_b, w_down_b, kept_mlp_b, gradient
    )
    grad_state, grad_gain_b1, grad_shift_b1 = norm_backward(
        state_four, gain_b[1], shift_b[1], grad_normed
    )
    gradient = gradient + grad_state
    grad_normed, grad_w_qkv_b, grad_w_out_b, grad_query_b, grad_value_b, grad_output_b = (
        self_backward(normed_fourth, w_qkv_b, w_out_b, allowed, kept_self_b, gradient)
    )
    grad_state, grad_gain_b0, grad_shift_b0 = norm_backward(
        state_three, gain_b[0], shift_b[0], grad_normed
    )
    gradient = gradient + grad_state
    grad_gains_b = jnp.stack([grad_gain_b0, grad_gain_b1])
    grad_biases_b = jnp.stack(
        [grad_shift_b0, grad_shift_b1, grad_query_b, grad_value_b, grad_output_b, grad_down_b]
    )
    owned_two = (
        lax.psum_scatter(grad_gains_b, ("dp", "fsdp"), scatter_dimension=1, tiled=True),
        lax.psum_scatter(grad_biases_b, ("dp", "fsdp"), scatter_dimension=1, tiled=True),
        lax.psum_scatter(flat_rows(grad_w_qkv_b), ("dp", "fsdp"), scatter_dimension=0, tiled=True),
        lax.psum_scatter(flat_rows(grad_w_out_b), ("dp", "fsdp"), scatter_dimension=0, tiled=True),
        lax.psum_scatter(flat_rows(grad_w_up_b), ("dp", "fsdp"), scatter_dimension=0, tiled=True),
        lax.psum_scatter(grad_bias_up_b, ("dp", "fsdp"), scatter_dimension=0, tiled=True),
        lax.psum_scatter(flat_rows(grad_w_down_b), ("dp", "fsdp"), scatter_dimension=0, tiled=True),
    )
    again_one = (
        lax.all_gather(gains_one, ("dp", "fsdp"), axis=1, tiled=True),
        lax.all_gather(biases_one, ("dp", "fsdp"), axis=1, tiled=True),
        lax.all_gather(w_qkv_one, ("dp", "fsdp"), axis=0, tiled=True),
        lax.all_gather(w_out_one, ("dp", "fsdp"), axis=0, tiled=True),
        lax.all_gather(w_cross_q, ("dp", "fsdp"), axis=0, tiled=True),
        lax.all_gather(w_cross_kv, ("dp", "fsdp"), axis=0, tiled=True),
        lax.all_gather(w_cross_out, ("dp", "fsdp"), axis=0, tiled=True),
        lax.all_gather(w_up_one, ("dp", "fsdp"), axis=0, tiled=True),
        lax.all_gather(bias_up_one, ("dp", "fsdp"), axis=0, tiled=True),
        lax.all_gather(w_down_one, ("dp", "fsdp"), axis=0, tiled=True),
    )
    (
        gains_a,
        biases_a,
        w_qkv_a,
        w_out_a,
        w_query_c,
        w_pair_c,
        w_out_c,
        w_up_a,
        bias_up_a,
        w_down_a,
    ) = again_one
    gain_a = gains_a.astype(jnp.float32)
    shift_a = biases_a.astype(jnp.float32)
    grad_normed, grad_w_up_a, grad_bias_up_a, grad_w_down_a, grad_down_a = mlp_backward(
        normed_third, w_up_a, w_down_a, kept_mlp_a, gradient
    )
    grad_state, grad_gain_a2, grad_shift_a2 = norm_backward(
        state_two, gain_a[2], shift_a[2], grad_normed
    )
    gradient = gradient + grad_state
    (
        grad_normed,
        grad_near,
        grad_w_query_c,
        grad_w_pair_c,
        grad_w_out_c,
        grad_query_c,
        grad_value_c,
        grad_output_c,
    ) = cross_backward(
        normed_second, near_rows, near_valid, w_query_c, w_pair_c, w_out_c, kept_cross, gradient
    )
    grad_state, grad_gain_a1, grad_shift_a1 = norm_backward(
        state_one, gain_a[1], shift_a[1], grad_normed
    )
    gradient = gradient + grad_state
    grad_normed, grad_w_qkv_a, grad_w_out_a, grad_query_a, grad_value_a, grad_output_a = (
        self_backward(normed_first, w_qkv_a, w_out_a, allowed, kept_self_a, gradient)
    )
    grad_state, grad_gain_a0, grad_shift_a0 = norm_backward(
        state_zero, gain_a[0], shift_a[0], grad_normed
    )
    gradient = gradient + grad_state
    grad_gains_a = jnp.stack([grad_gain_a0, grad_gain_a1, grad_gain_a2])
    grad_biases_a = jnp.stack(
        [
            grad_shift_a0,
            grad_shift_a1,
            grad_shift_a2,
            grad_query_a,
            grad_value_a,
            grad_output_a,
            grad_query_c,
            grad_value_c,
            grad_output_c,
            grad_down_a,
        ]
    )
    grad_neighbours = jnp.zeros((store_count, near_length, model_width), jnp.float32)
    grad_neighbours = grad_neighbours.at[near_index].add(
        grad_near.reshape(span_count * near_count, near_length, model_width)
    )
    owned_one = (
        lax.psum_scatter(grad_gains_a, ("dp", "fsdp"), scatter_dimension=1, tiled=True),
        lax.psum_scatter(grad_biases_a, ("dp", "fsdp"), scatter_dimension=1, tiled=True),
        lax.psum_scatter(flat_rows(grad_w_qkv_a), ("dp", "fsdp"), scatter_dimension=0, tiled=True),
        lax.psum_scatter(flat_rows(grad_w_out_a), ("dp", "fsdp"), scatter_dimension=0, tiled=True),
        lax.psum_scatter(
            flat_rows(grad_w_query_c), ("dp", "fsdp"), scatter_dimension=0, tiled=True
        ),
        lax.psum_scatter(flat_rows(grad_w_pair_c), ("dp", "fsdp"), scatter_dimension=0, tiled=True),
        lax.psum_scatter(flat_rows(grad_w_out_c), ("dp", "fsdp"), scatter_dimension=0, tiled=True),
        lax.psum_scatter(flat_rows(grad_w_up_a), ("dp", "fsdp"), scatter_dimension=0, tiled=True),
        lax.psum_scatter(grad_bias_up_a, ("dp", "fsdp"), scatter_dimension=0, tiled=True),
        lax.psum_scatter(flat_rows(grad_w_down_a), ("dp", "fsdp"), scatter_dimension=0, tiled=True),
    )
    return (
        state_five.astype(jnp.bfloat16),
        gradient,
        grad_neighbours,
        owned_one[0],
        owned_one[1],
        restore_rows(owned_one[2], 3 * model_width),
        restore_rows(owned_one[3], model_width),
        restore_rows(owned_one[4], model_width),
        restore_rows(owned_one[5], 2 * model_width),
        restore_rows(owned_one[6], model_width),
        restore_rows(owned_one[7], hidden_width),
        owned_one[8],
        restore_rows(owned_one[9], model_width),
        owned_two[0],
        owned_two[1],
        restore_rows(owned_two[2], 3 * model_width),
        restore_rows(owned_two[3], model_width),
        restore_rows(owned_two[4], hidden_width),
        owned_two[5],
        restore_rows(owned_two[6], model_width),
    )


def solution(mesh):
    in_specs = (
        P(("dp", "fsdp"), None),
        P(("dp", "fsdp"), None),
        P(("dp", "fsdp"), None, None),
        P(("dp", "fsdp"), None, None),
        P(("dp", "fsdp"), None),
        P(None, ("dp", "fsdp")),
        P(None, ("dp", "fsdp")),
        P(("dp", "fsdp"), None),
        P(("dp", "fsdp"), None),
        P(("dp", "fsdp"), None),
        P(("dp", "fsdp"), None),
        P(("dp", "fsdp"), None),
        P(("dp", "fsdp"), None),
        P(("dp", "fsdp")),
        P(("dp", "fsdp"), None),
        P(None, ("dp", "fsdp")),
        P(None, ("dp", "fsdp")),
        P(("dp", "fsdp"), None),
        P(("dp", "fsdp"), None),
        P(("dp", "fsdp"), None),
        P(("dp", "fsdp")),
        P(("dp", "fsdp"), None),
        P(("dp", "fsdp"), None),
    )
    out_specs = (
        P(("dp", "fsdp"), None),
        P(("dp", "fsdp"), None),
        P(("dp", "fsdp"), None, None),
        P(None, ("dp", "fsdp")),
        P(None, ("dp", "fsdp")),
        P(("dp", "fsdp"), None),
        P(("dp", "fsdp"), None),
        P(("dp", "fsdp"), None),
        P(("dp", "fsdp"), None),
        P(("dp", "fsdp"), None),
        P(("dp", "fsdp"), None),
        P(("dp", "fsdp")),
        P(("dp", "fsdp"), None),
        P(None, ("dp", "fsdp")),
        P(None, ("dp", "fsdp")),
        P(("dp", "fsdp"), None),
        P(("dp", "fsdp"), None),
        P(("dp", "fsdp"), None),
        P(("dp", "fsdp")),
        P(("dp", "fsdp"), None),
    )
    return jax.shard_map(local, mesh=mesh, in_specs=in_specs, out_specs=out_specs, check_vma=False)
```

profile of v0, /device:TPU:0, one launch (start us, length us, event | category | flops | bytes accessed | tf_op | source)
XLA Modules:
  0.0 2261.3 jit_solution(3155758277207344991)
XLA Ops:
  16.4 71.1 %all-gather.1 = bf16[32,24,10]{1,2,0:T(8,128)(2,1)S(1)} all-gather(bf16[1,24,10]{1,2,0:T(8,128)(2,1)} %bitcast.258), channel_id=1, replica_groups=mesh['dp'=4,'fsdp'=8] {'dp','fsdp'}, dimensions={0}, use_global_device_ids=true | all-gather | bytes 15840 | tf_op jit(solution)/shard_map/all_gather | solution.py:276
  88.3 64.4 %all-gather.3 = bf16[32,24,6]{1,2,0:T(8,128)(2,1)S(1)} all-gather(bf16[1,24,6]{1,2,0:T(8,128)(2,1)} %bitcast.260), channel_id=1, replica_groups=mesh['dp'=4,'fsdp'=8] {'dp','fsdp'}, dimensions={0}, use_global_device_ids=true | all-gather | bytes 9504 | tf_op jit(solution)/shard_map/all_gather | solution.py:324
  153.6 65.9 %all-gather = bf16[32,24,3]{1,2,0:T(4,128)(2,1)S(1)} all-gather(bf16[1,24,3]{1,2,0:T(4,128)(2,1)} %bitcast.261), channel_id=1, replica_groups=mesh['dp'=4,'fsdp'=8] {'dp','fsdp'}, dimensions={0}, use_global_device_ids=true | all-gather | bytes 4752 | tf_op jit(solution)/shard_map/all_gather | solution.py:275
  226.6 37.2 %all-reduce.10 = (bf16[3072]{0:T(1024)(128)(2,1)S(1)}, bf16[3072]{0:T(1024)(128)(2,1)S(1)}) all-reduce(bf16[3072]{0:T(1024)(128)(2,1)S(1)} %dynamic-update-slice, bf16[3072]{0:T(1024)(128)(2,1)S(1)} %dynamic-update-slice.1), channel_id=1, replica_groups=mesh['dp'=4,'fsdp'=8] {'dp','fsdp'}, use_global_device_ids=true, to_apply=%add.1 | all-reduce | flops 6144 | bytes 24576
  264.4 65.4 %all-gather.2 = bf16[32,24,2]{1,2,0:T(2,128)(2,1)S(1)} all-gather(bf16[1,24,2]{1,2,0:T(2,128)(2,1)S(1)} %bitcast.262), channel_id=1, replica_groups=mesh['dp'=4,'fsdp'=8] {'dp','fsdp'}, dimensions={0}, use_global_device_ids=true | all-gather | bytes 3168 | tf_op jit(solution)/shard_map/all_gather | solution.py:323
  333.5 5.8 add_convert_fusion
  339.3 4.6 copy.141
  343.9 5.0 reshape.574
  348.9 3.0 fusion.120
  352.0 3.2 fusion
  365.9 2.7 fusion.125
  372.8 2.9 reshape.576
  381.2 5.7 convolution_add_fusion.3
  386.9 45.9 %all-gather.28.cloned.1.call-done = bf16[3072,768]{1,0:T(8,128)(2,1)} async-done(((bf16[96,768]{1,0:T(8,128)(2,1)}), bf16[3072,768]{1,0:T(8,128)(2,1)}) %all-gather.28.cloned.1.call-update) | async-done | bytes 4718608 | tf_op jit(solution)/shard_map/all_gather | solution.py:284
  432.8 5.5 fusion.127
  440.6 54.2 %all-gather.30.cloned.1.call-done = bf16[768,2304]{1,0:T(8,128)(2,1)} async-done(((bf16[24,2304]{1,0:T(8,128)(2,1)}), bf16[768,2304]{1,0:T(8,128)(2,1)}) %all-gather.30.cloned.1.call-update) | async-done | bytes 3538960 | tf_op jit(solution)/shard_map/all_gather | solution.py:325
  494.8 4.5 fusion.1
  508.3 42.5 %all-gather.32.cloned.1.call-done = bf16[768,768]{1,0:T(8,128)(2,1)} async-done(((bf16[24,768]{1,0:T(8,128)(2,1)}), bf16[768,768]{1,0:T(8,128)(2,1)}) %all-gather.32.cloned.1.call-update) | async-done | bytes 1179664 | tf_op jit(solution)/shard_map/all_gather | solution.py:326
  555.3 60.9 %all-gather.36.cloned.1.call-done = bf16[3072,768]{1,0:T(8,128)(2,1)} async-done(((bf16[96,768]{1,0:T(8,128)(2,1)}), bf16[3072,768]{1,0:T(8,128)(2,1)}) %all-gather.36.cloned.1.call-update) | async-done | bytes 4718608 | tf_op jit(solution)/shard_map/all_gather | solution.py:329
  616.3 5.6 fusion.130
  621.8 60.0 %all-gather.34.cloned.1.call-done = bf16[768,3072]{1,0:T(8,128)(2,1)} async-done(((bf16[24,3072]{1,0:T(8,128)(2,1)}), bf16[768,3072]{1,0:T(8,128)(2,1)}) %all-gather.34.cloned.1.call-update) | async-done | bytes 4718608 | tf_op jit(solution)/shard_map/all_gather | solution.py:327
  681.8 9.6 convert_reduce_fusion
  711.9 3.8 convert_reduce_fusion.1
  726.2 3.1 multiply_reduce_fusion.1
  737.8 3.1 multiply_reduce_fusion.6
  746.2 2.8 fusion.42
  759.0 2.9 copy.165
  789.6 3.2 fusion.94
  792.8 3.2 reshape.591
  796.1 3.3 fusion.107
  799.5 3.2 reshape.593
  802.8 3.0 fusion.132
  805.8 3.2 reshape.597
  809.1 3.0 fusion.133
  812.1 3.2 reshape.609
  817.8 4.4 fusion.131
  822.2 5.6 reshape.595
  828.5 5.5 fusion.103
  834.0 7.9 reshape.589
  842.6 5.7 fusion.109
  848.4 7.9 reshape.607
  857.0 6.9 fusion.108
  863.9 11.0 reshape.599
  875.0 8.0 fusion.97
  883.0 10.8 reshape.601
  894.4 6.9 fusion.110
  901.4 10.9 reshape.611
  912.3 7.8 fusion.111
  920.1 10.9 reshape.613
  931.0 3.2 convert_element_type.292
  934.2 7.0 fusion.16
  943.2 8.1 scatter_fusion
  952.6 6.2 fusion.55
  966.7 50.5 %reduce-scatter.18.cloned.1.call-done = f32[144,128]{1,0:T(8,128)} async-done(((f32[4608,128]{1,0:T(8,128)}), f32[144,128]{1,0:T(8,128)}) %reduce-scatter.18.cloned.1.call-update) | async-done | bytes 73744 | tf_op jit(solution)/shard_map/reduce_scatter | solution.py:461
  1018.7 102.5 %reduce-scatter.20.cloned.1.call-done = f32[144,128]{1,0:T(8,128)} async-done(((f32[4608,128]{1,0:T(8,128)}), f32[144,128]{1,0:T(8,128)}) %reduce-scatter.20.cloned.1.call-update) | async-done | bytes 73744 | tf_op jit(solution)/shard_map/reduce_scatter | solution.py:462
  1122.7 101.8 %reduce-scatter.24.cloned.1.call-done = f32[144,128]{1,0:T(8,128)} async-done(((f32[4608,128]{1,0:T(8,128)}), f32[144,128]{1,0:T(8,128)}) %reduce-scatter.24.cloned.1.call-update) | async-done | bytes 73744 | tf_op jit(solution)/shard_map/reduce_scatter | solution.py:466
  1226.1 102.5 %reduce-scatter.32.cloned.1.call-done = f32[144,128]{1,0:T(8,128)} async-done(((f32[4608,128]{1,0:T(8,128)}), f32[144,128]{1,0:T(8,128)}) %reduce-scatter.32.cloned.1.call-update) | async-done | bytes 73744 | tf_op jit(solution)/shard_map/reduce_scatter | solution.py:377
  1330.0 109.8 %reduce-scatter.22.cloned.1.call-done = f32[288,128]{1,0:T(8,128)} async-done(((f32[9216,128]{1,0:T(8,128)}), f32[288,128]{1,0:T(8,128)}) %reduce-scatter.22.cloned.1.call-update) | async-done | bytes 147472 | tf_op jit(solution)/shard_map/reduce_scatter | solution.py:465
  1441.5 123.1 %reduce-scatter.16.cloned.1.call-done = f32[432,128]{1,0:T(8,128)} async-done(((f32[13824,128]{1,0:T(8,128)}), f32[432,128]{1,0:T(8,128)}) %reduce-scatter.16.cloned.1.call-update) | async-done | bytes 221200 | tf_op jit(solution)/shard_map/reduce_scatter | solution.py:460
  1566.2 122.4 %reduce-scatter.30.cloned.1.call-done = f32[432,128]{1,0:T(8,128)} async-done(((f32[13824,128]{1,0:T(8,128)}), f32[432,128]{1,0:T(8,128)}) %reduce-scatter.30.cloned.1.call-update) | async-done | bytes 221200 | tf_op jit(solution)/shard_map/reduce_scatter | solution.py:376
  1690.2 139.7 %reduce-scatter.26.cloned.1.call-done = f32[576,128]{1,0:T(8,128)} async-done(((f32[18432,128]{1,0:T(8,128)}), f32[576,128]{1,0:T(8,128)}) %reduce-scatter.26.cloned.1.call-update) | async-done | bytes 294928 | tf_op jit(solution)/shard_map/reduce_scatter | solution.py:467
  1831.6 139.0 %reduce-scatter.28.cloned.1.call-done = f32[576,128]{1,0:T(8,128)} async-done(((f32[18432,128]{1,0:T(8,128)}), f32[576,128]{1,0:T(8,128)}) %reduce-scatter.28.cloned.1.call-update) | async-done | bytes 294928 | tf_op jit(solution)/shard_map/reduce_scatter | solution.py:469
  1972.3 140.0 %reduce-scatter.34.cloned.1.call-done = f32[576,128]{1,0:T(8,128)} async-done(((f32[18432,128]{1,0:T(8,128)}), f32[576,128]{1,0:T(8,128)}) %reduce-scatter.34.cloned.1.call-update) | async-done | bytes 294928 | tf_op jit(solution)/shard_map/reduce_scatter | solution.py:378
  2114.1 138.7 %reduce-scatter.36.cloned.1.call-done = f32[576,128]{1,0:T(8,128)} async-done(((f32[18432,128]{1,0:T(8,128)}), f32[576,128]{1,0:T(8,128)}) %reduce-scatter.36.cloned.1.call-update) | async-done | bytes 294928 | tf_op jit(solution)/shard_map/reduce_scatter | solution.py:380
  (528 shorter events, 174.0 us)
Async XLA Ops:
  7.2 217.6 %copy-start = (bf16[8,128,768]{2,1,0:T(8,128)(2,1)S(1)}, bf16[8,128,768]{2,1,0:T(8,128)(2,1)}, u32[]{:S(2)}) copy-start(bf16[8,128,768]{2,1,0:T(8,128)(2,1)} %param.25) | copy-start | bytes 4718596
  7.2 218.2 %copy-start.58 = (s32[8,128]{1,0:T(8,128)S(1)}, s32[8,128]{1,0:T(8,128)}, u32[]{:S(2)}) copy-start(s32[8,128]{1,0:T(8,128)} %param.27) | copy-start | bytes 12292
  7.2 218.9 %copy-start.144 = (bf16[96]{0:T(256)(128)(2,1)S(1)}, bf16[96]{0:T(256)(128)(2,1)}, u32[]{:S(2)}) copy-start(bf16[96]{0:T(256)(128)(2,1)} %param.36) | copy-start | bytes 580
  7.2 219.1 %copy-start.145 = (bf16[96]{0:T(256)(128)(2,1)S(1)}, bf16[96]{0:T(256)(128)(2,1)}, u32[]{:S(2)}) copy-start(bf16[96]{0:T(256)(128)(2,1)} %param.43) | copy-start | bytes 580
  7.2 257.2 %copy-start.138 = (bf16[2,24]{1,0:T(2,128)(2,1)S(1)}, bf16[2,24]{1,0:T(2,128)(2,1)}, u32[]{:S(2)}) copy-start(bf16[2,24]{1,0:T(2,128)(2,1)} %param.38) | copy-start | bytes 292
  7.2 326.2 %all-gather.20.cloned.1.call-start = ((), (), s32[]{:S(2)}) async-start(), calls=%async_computation.13 | async-start | bytes 2433024 | tf_op jit(solution)/shard_map/all_gather | solution.py:280
  8.0 344.0 %all-gather.16.cloned.1.call-start = ((), (), s32[]{:S(2)}) async-start(), calls=%async_computation.11 | async-start | bytes 3649536 | tf_op jit(solution)/shard_map/all_gather | solution.py:277
  8.7 350.3 %all-gather.18.cloned.1.call-start = ((), (), s32[]{:S(2)}) async-start(), calls=%async_computation.12 | async-start | bytes 1216512 | tf_op jit(solution)/shard_map/all_gather | solution.py:278
  9.5 351.9 %all-gather.22.cloned.1.call-start = ((), (), s32[]{:S(2)}) async-start(), calls=%async_computation.14 | async-start | bytes 1216512 | tf_op jit(solution)/shard_map/all_gather | solution.py:279
  10.0 365.7 %all-gather.24.cloned.1.call-start = ((), (), s32[]{:S(2)}) async-start(), calls=%async_computation.15 | async-start | bytes 1216512 | tf_op jit(solution)/shard_map/all_gather | solution.py:281
  10.6 370.5 %all-gather.26.cloned.1.call-start = ((), (), s32[]{:S(2)}) async-start(), calls=%async_computation.16 | async-start | bytes 4866048 | tf_op jit(solution)/shard_map/all_gather | solution.py:282
  11.2 421.6 %all-gather.28.cloned.1.call-start = ((), (), s32[]{:S(2)}) async-start(), calls=%async_computation.17 | async-start | bytes 4866048 | tf_op jit(solution)/shard_map/all_gather | solution.py:284
  12.0 482.8 %all-gather.30.cloned.1.call-start = ((), (), s32[]{:S(2)}) async-start(), calls=%async_computation.18 | async-start | bytes 3649536 | tf_op jit(solution)/shard_map/all_gather | solution.py:325
  12.7 538.1 %all-gather.32.cloned.1.call-start = ((), (), s32[]{:S(2)}) async-start(), calls=%async_computation.19 | async-start | bytes 1216512 | tf_op jit(solution)/shard_map/all_gather | solution.py:326
  13.4 602.8 %all-gather.36.cloned.1.call-start = ((), (), s32[]{:S(2)}) async-start(), calls=%async_computation.21 | async-start | bytes 4866048 | tf_op jit(solution)/shard_map/all_gather | solution.py:329
  14.0 667.7 %all-gather.34.cloned.1.call-start = ((), (), s32[]{:S(2)}) async-start(), calls=%async_computation.20 | async-start | bytes 4866048 | tf_op jit(solution)/shard_map/all_gather | solution.py:327
  14.8 944.0 %all-reduce.13.cloned.1.call-start = ((), (), s32[]{:S(2)}) async-start(), calls=%async_computation.33 | async-start | bytes 233472
  220.9 131.1 %copy-start.82 = (f32[256]{0:T(256)}, f32[256]{0:T(256)S(1)}, u32[]{:S(2)}) copy-start(f32[256]{0:T(256)S(1)} %broadcast_multiply_fusion.4) | copy-start | bytes 3076
  225.5 113.8 %copy-start.11 = (bf16[8,128,768]{2,1,0:T(8,128)(2,1)}, bf16[8,128,768]{2,1,0:T(8,128)(2,1)S(1)}, u32[]{:S(2)}) copy-start(bf16[8,128,768]{2,1,0:T(8,128)(2,1)S(1)} %gather_fusion) | copy-start | bytes 4718596
  331.3 20.7 copy-start.59
  331.3 20.7 copy-start.72
  331.3 30.0 %copy-start.84 = (f32[768]{0:T(1024)}, f32[768]{0:T(1024)S(1)}, u32[]{:S(2)}) copy-start(f32[768]{0:T(1024)S(1)} %get-tuple-element.130) | copy-start | bytes 9220
  361.0 4.8 copy-start.6
  361.0 4.8 copy-start.96
  361.3 7.3 copy-start.111
  369.5 6.3 copy-start.99
  375.8 4.7 copy-start.56
  375.8 4.7 copy-start.68
  681.8 9.6 copy-start.17
  681.8 9.6 copy-start.61
  681.8 9.6 copy-start.93
  681.8 9.6 copy-start.105
  681.8 9.6 copy-start.141
  706.8 4.5 slice-start.2
  710.3 5.3 slice-start
  711.2 7.1 copy-start.12
  758.7 4.5 copy-start.48
  758.7 4.4 copy-start.109
  759.0 6.3 copy-start.134
  759.0 6.9 copy-start.132
  771.7 4.9 copy-start.129
  771.7 5.5 copy-start.131
  771.7 6.0 copy-start.130
  771.7 6.6 copy-start.128
  771.8 7.2 copy-start.74
  789.6 227.6 %reduce-scatter.18.cloned.1.call-start = ((), (), s32[]{:S(2)}) async-start(), calls=%async_computation.23 | async-start | bytes 2433024 | tf_op jit(solution)/shard_map/reduce_scatter | solution.py:461
  796.0 325.1 %reduce-scatter.20.cloned.1.call-start = ((), (), s32[]{:S(2)}) async-start(), calls=%async_computation.24 | async-start | bytes 2433024 | tf_op jit(solution)/shard_map/reduce_scatter | solution.py:462
  802.7 421.8 %reduce-scatter.24.cloned.1.call-start = ((), (), s32[]{:S(2)}) async-start(), calls=%async_computation.26 | async-start | bytes 2433024 | tf_op jit(solution)/shard_map/reduce_scatter | solution.py:466
  809.0 519.5 %reduce-scatter.32.cloned.1.call-start = ((), (), s32[]{:S(2)}) async-start(), calls=%async_computation.30 | async-start | bytes 2433024 | tf_op jit(solution)/shard_map/reduce_scatter | solution.py:377
  815.3 624.5 %reduce-scatter.22.cloned.1.call-start = ((), (), s32[]{:S(2)}) async-start(), calls=%async_computation.25 | async-start | bytes 4866048 | tf_op jit(solution)/shard_map/reduce_scatter | solution.py:465
  827.8 736.7 %reduce-scatter.16.cloned.1.call-start = ((), (), s32[]{:S(2)}) async-start(), calls=%async_computation.22 | async-start | bytes 7299072 | tf_op jit(solution)/shard_map/reduce_scatter | solution.py:460
  842.0 846.6 %reduce-scatter.30.cloned.1.call-start = ((), (), s32[]{:S(2)}) async-start(), calls=%async_computation.29 | async-start | bytes 7299072 | tf_op jit(solution)/shard_map/reduce_scatter | solution.py:376
  856.3 973.6 %reduce-scatter.26.cloned.1.call-start = ((), (), s32[]{:S(2)}) async-start(), calls=%async_computation.27 | async-start | bytes 9732096 | tf_op jit(solution)/shard_map/reduce_scatter | solution.py:467
  874.9 1095.7 %reduce-scatter.28.cloned.1.call-start = ((), (), s32[]{:S(2)}) async-start(), calls=%async_computation.28 | async-start | bytes 9732096 | tf_op jit(solution)/shard_map/reduce_scatter | solution.py:469
  893.8 1218.5 %reduce-scatter.34.cloned.1.call-start = ((), (), s32[]{:S(2)}) async-start(), calls=%async_computation.31 | async-start | bytes 9732096 | tf_op jit(solution)/shard_map/reduce_scatter | solution.py:378
  912.3 1340.5 %reduce-scatter.36.cloned.1.call-start = ((), (), s32[]{:S(2)}) async-start(), calls=%async_computation.32 | async-start | bytes 9732096 | tf_op jit(solution)/shard_map/reduce_scatter | solution.py:380
  943.2 8.2 copy-start.125
  943.2 8.2 copy-start.15
  943.2 8.2 copy-start.49
  943.2 8.2 copy-start.89
  943.2 8.2 copy-start.110
  943.2 9.4 copy-start.18
  943.2 9.4 copy-start.126
  952.6 1302.0 %copy-start.1 = (bf16[8,128,768]{2,1,0:T(8,128)(2,1)S(1)}, bf16[8,128,768]{2,1,0:T(8,128)(2,1)}, u32[]{:S(2)}) copy-start(bf16[8,128,768]{2,1,0:T(8,128)(2,1)} %param.25) | copy-start | bytes 4718596
  (109 other events, 231.3 us)
Sparse Core Ops, SparseCore 0:
  11.1 60.2 all-gather.19
  74.4 59.1 all-gather.15
  136.6 53.0 all-gather.17
  192.5 53.1 all-gather.21
  248.5 53.1 all-gather.23
  304.6 62.6 all-gather.25
  370.2 62.4 all-gather.27
  435.8 58.9 all-gather.29
  497.8 52.9 all-gather.31
  553.6 62.6 all-gather.35
  619.2 62.4 all-gather.33
  789.7 123.1 all-reduce.12
  918.2 98.9 reduce-scatter.17
  1023.2 97.9 reduce-scatter.19
  1126.3 98.1 reduce-scatter.23
  1230.5 97.9 reduce-scatter.31
  1333.8 105.9 reduce-scatter.21
  1446.4 118.1 reduce-scatter.15
  1570.2 118.3 reduce-scatter.29
  1695.3 134.5 reduce-scatter.25
  1835.8 134.7 reduce-scatter.27
  1977.5 134.7 reduce-scatter.33
  2118.2 134.5 reduce-scatter.35
where the time goes:
time: 2270 us; the launch traced here: 2260 us
  waiting for transfers between devices  1540 us (68%)
  blocking collectives  304 us (13%)
  local copies, waits for them, and re-layouts  195 us (9%)
  matrix products  165 us (7%)
  other arithmetic  40 us (2%)
    reduce_scatter x1, waiting for transfers between devices, local(): lax.psum_scatter(flat_rows(grad_w_up_b), ('dp', 'fsdp'), scatter_dimensio...  140 us
    reduce_scatter x1, waiting for transfers between devices, local(): lax.psum_scatter(flat_rows(grad_w_up_a), ('dp', 'fsdp'), scatter_dimensio...  140 us
    reduce_scatter x1, waiting for transfers between devices, local(): lax.psum_scatter(flat_rows(grad_w_down_a), ('dp', 'fsdp'), scatter_dimens...  139 us
    reduce_scatter x1, waiting for transfers between devices, local(): lax.psum_scatter(flat_rows(grad_w_down_b), ('dp', 'fsdp'), scatter_dimens...  139 us
    dot_general x33, matrix products, product(): return jnp.dot(left, right, preferred_element_type=jnp.float32)  137 us
    reduce_scatter x1, waiting for transfers between devices, local(): lax.psum_scatter(flat_rows(grad_w_qkv_a), ('dp', 'fsdp'), scatter_dimensi...  123 us
    reduce_scatter x1, waiting for transfers between devices, local(): lax.psum_scatter(flat_rows(grad_w_qkv_b), ('dp', 'fsdp'), scatter_dimensi...  122 us
    reduce_scatter x1, waiting for transfers between devices, local(): lax.psum_scatter(flat_rows(grad_w_pair_c), ('dp', 'fsdp'), scatter_dimens...  110 us
  transfers between devices with their start and end apart: 23, of which 16 were waited for; matrix products, arithmetic and copies ran while one was open for 12% of the time, Pallas kernels for 0%

commit v1 on v0

v1 whole, which is shorter than its diff:
```python
import functools
import itertools
import math
import types
import jax
import jax.numpy as jnp
from jax import lax
from jax.experimental import pallas as pl
from jax.experimental.pallas import tpu as pltpu
from jax.sharding import PartitionSpec as P

HEADS = 12
HEAD_DIM = 64
MESH = pl.DeviceIdType.MESH
ROUTES = ((("z", "x", "y"), 1), (("z", "y", "x"), 1), (("x", "z", "y"), 2), (("y", "z", "x"), 2))
NAMES = ("y", "c", "z", "x")
GATHER_STEPS = (0, 1, 2, 3, 4, 6, 8)
VMEM_MOST = 63 * 2 ** 20
COMPUTE_SHARE, CHAIN_SHARE = 3.5, 3.0
SCATTER_STEPS = (0, 2, 4, 5, 6, 7, 8)
LANDINGS, WINDOW = 6, 8


class Place:
    def __init__(self, dp_size, fsdp_size):
        dp, fsdp = lax.axis_index("dp"), lax.axis_index("fsdp")
        self.size = {"y": dp_size // 2, "c": 2, "z": fsdp_size // 2, "x": 2}
        self.at = {"y": dp // 2, "c": lax.rem(dp, 2), "z": fsdp // 2, "x": lax.rem(fsdp, 2)}

    def device(self, axis, index):
        at = dict(self.at)
        at[axis] = index
        return (at["y"] * 2 + at["c"], at["z"] * 2 + at["x"])

    def partners(self):
        found = []
        for axis in ("c", "x", "y", "z"):
            n, p = self.size[axis], self.at[axis]
            if n == 2:
                found.append((self.device(axis, 1 - p), None))
            elif n > 2:
                found.append((self.device(axis, p + 1), p + 1 < n))
                found.append((self.device(axis, p - 1), p > 0))
        return found


def greet(place):
    barrier = pltpu.get_barrier_semaphore()
    expected = 0
    for device, condition in place.partners():
        if condition is None:
            pl.semaphore_signal(barrier, inc=1, device_id=device, device_id_type=MESH)
            expected = expected + 1
        else:
            @pl.when(condition)
            def _(device=device):
                pl.semaphore_signal(barrier, inc=1, device_id=device, device_id_type=MESH)
            expected = expected + condition.astype(jnp.int32)
    pl.semaphore_wait(barrier, expected)


def when(condition, action):
    if condition is None:
        action()
    else:
        pl.when(condition)(action)


class Sems:
    def __init__(self, send, recv):
        self.send, self.recv, self.used, self.sent = send, recv, 0, []

    def take(self):
        self.used += 1
        return self.used - 1

    def copy(self, slot, src, dst, device):
        return pltpu.make_async_remote_copy(
            src_ref=src, dst_ref=dst, send_sem=self.send.at[slot], recv_sem=self.recv.at[slot],
            device_id=device, device_id_type=MESH)

    def start(self, slot, src, dst, device, condition=None):
        copy = self.copy(slot, src, dst, device)
        when(condition, copy.start)
        self.sent.append((copy, condition))

    def arrived(self, slot, dst, device, condition=None):
        when(condition, self.copy(slot, dst, dst, device).wait_recv)

    def drain(self):
        for copy, condition in self.sent:
            when(condition, copy.wait_send)


def run_schedule(groups, offsets, after=None):
    for tick in range(len(groups) + offsets[-1]):
        for k, group in enumerate(groups):
            if tick - k in offsets:
                for flow in group:
                    next(flow, None)
        if after is not None:
            after(tick)


def routes(width):
    if width % 768:
        return [(ROUTES[0][0], 0, width)]
    found, start = [], 0
    for order, share in ROUTES:
        found.append((order, start, share * width // 6))
        start += share * width // 6
    return found


def copies_of(order, size):
    return 1 + sum(1 if size[d] == 2 else 2 * (size[d] - 1) for d in order)


def gather_flow(place, sems, ref, order, row, height, col, width):
    part = (pl.ds(row, height), pl.ds(col, width))

    def block(done, **fixed):
        where = []
        for name in NAMES:
            if name in fixed:
                where.append(fixed[name])
            elif name in done:
                where.append(pl.ds(0, place.size[name]))
            else:
                where.append(place.at[name])
        return ref.at[(*where, *part)]

    c = place.at["c"]
    sibling = place.device("c", 1 - c)
    done, crossed = set(), []

    def cross(**fixed):
        slot, mine = sems.take(), block(done, c=c, **fixed)
        sems.start(slot, mine, mine, sibling)
        crossed.append((slot, block(done, c=1 - c, **fixed)))

    for axis in order:
        n, p = place.size[axis], place.at[axis]
        final = axis == order[-1]
        if n == 2:
            slot, other = sems.take(), place.device(axis, 1 - p)
            mine = block(done, **{axis: p})
            sems.start(slot, mine, mine, other)
            if final:
                cross(**{axis: p})
            yield
            sems.arrived(slot, block(done, **{axis: 1 - p}), other)
            if final:
                cross(**{axis: 1 - p})
        else:
            for step in range(n - 1):
                up, down = sems.take(), sems.take()
                above, below = place.device(axis, p + 1), place.device(axis, p - 1)
                sent = block(done, **{axis: jnp.maximum(p - step, 0)})
                sems.start(up, sent, sent, above, (p - step >= 0) & (p + 1 < n))
                sent = block(done, **{axis: jnp.minimum(p + step, n - 1)})
                sems.start(down, sent, sent, below, (p + step < n) & (p > 0))
                yield
                sems.arrived(up, block(done, **{axis: jnp.maximum(p - 1 - step, 0)}), above, p - 1 - step >= 0)
                sems.arrived(down, block(done, **{axis: jnp.minimum(p + 1 + step, n - 1)}), below, p + 1 + step < n)
            done.add(axis)
            if final:
                cross()
            continue
        done.add(axis)
    yield
    for slot, theirs in crossed:
        sems.arrived(slot, theirs, sibling)


def pack_small(parts, ups):
    rows = [jnp.pad(ref[...].astype(jnp.float32), ((0, 0), (0, 128 - ref.shape[1]))) for ref in (*parts, *ups)]
    rows = jnp.concatenate(rows, axis=0)
    return jnp.pad(rows, ((0, -rows.shape[0] % 32), (0, 0))).astype(jnp.bfloat16)


def add_blocks(lead, result, *terms):
    def body(where):
        kind = F32 if isinstance(result, list) else result.dtype
        total = terms[0][where].astype(kind)
        for term in terms[1:]:
            total = total + term[where].astype(kind)
        if isinstance(result, list):
            result[where[0]][...] = total
        else:
            result[where] = total

    for index in itertools.product(*map(range, lead)):
        body((*index, slice(None), slice(None)))


def scatter_buffers(size, order, block):
    dims, found = [name for name in NAMES if name != "c"], []
    for axis in order:
        dims = [name for name in dims if name != axis]
        lead = tuple(size[name] for name in dims)
        found.append((() if size[axis] == 2 else (2 * size[axis] - 2,)) + lead + block)
    return found


def scatter_flow(place, sems, sums, buffers, order, out, parts):
    dims = [name for name in NAMES if name != "c"]
    leaving = []

    def leave(slot, src, dst, device, condition=None):
        copy = sems.copy(slot, src, dst, device)
        when(condition, copy.start)
        leaving.append((copy, condition))

    def settle():
        while leaving:
            copy, condition = leaving.pop()
            when(condition, copy.wait_send)

    for axis, buffer in zip(order, buffers):
        n, p = place.size[axis], place.at[axis]
        spot = dims.index(axis)
        rest = [name for name in dims if name != axis]
        lead = tuple(place.size[name] for name in rest) + parts
        last = not rest

        def at(index, sums=sums, spot=spot, count=len(dims)):
            where = [slice(None)] * (count + 3)
            where[spot] = index
            return sums.at[tuple(where)]

        if n == 2:
            slot, other = sems.take(), place.device(axis, 1 - p)
            leave(slot, at(1 - p), buffer, other)
            yield
            sems.arrived(slot, buffer, other)
            settle()
            add_blocks(lead, out if last else buffer, buffer, at(p))
            sums = buffer
        else:
            above, below = place.device(axis, p + 1), place.device(axis, p - 1)
            q = n - 1 - p
            ups = [sems.take() for _ in range(n - 1)]
            downs = [sems.take() for _ in range(n - 1)]

            def from_below(block):
                return buffer.at[jnp.maximum(block - 1, 0)]

            def from_above(block):
                return buffer.at[jnp.minimum(n - 1 + block, 2 * n - 3)]
            for step in range(n - 1):
                up = jnp.minimum(n - 1 - step + p, n - 1)
                down = jnp.maximum(step - q, 0)
                if step:
                    def pass_up(up=up, step=step):
                        sems.copy(ups[step - 1], from_below(up), from_below(up), above).wait_recv()
                        add_blocks(lead, at(up), at(up), from_below(up))
                    def pass_down(down=down, step=step):
                        sems.copy(downs[step - 1], from_above(down), from_above(down), below).wait_recv()
                        add_blocks(lead, at(down), at(down), from_above(down))
                    pl.when((step >= p) & (p > 0) & (p < n - 1))(pass_up)
                    pl.when((step >= q) & (q > 0) & (q < n - 1))(pass_down)
                leave(ups[step], at(up), from_below(up), above, (step >= p) & (p < n - 1))
                leave(downs[step], at(down), from_above(down), below, (step >= q) & (p > 0))
                yield
            sems.arrived(ups[n - 2], from_below(p), above, p > 0)
            sems.arrived(downs[n - 2], from_above(p), below, p < n - 1)
            settle()
            result = out if last else at(p)
            pl.when(p == 0)(lambda: add_blocks(lead, result, at(p), from_above(p)))
            pl.when(p == n - 1)(lambda: add_blocks(lead, result, at(p), from_below(p)))
            pl.when((p > 0) & (p < n - 1))(
                lambda: add_blocks(lead, result, at(p), from_below(p), from_above(p)))
            sums = at(p)
        dims = rest


def split_kernel(D, *refs):
    one, up_one, down_one, two, up_two, down_two, small, near_in, ids = refs[:9]
    (gains_a, biases_a, qkv_a, out_a, cross_q, cross_kv, cross_out, g_up_a, bias_up_a, g_down_a,
     gains_b, biases_b, qkv_b, out_b, g_up_b, bias_up_b, g_down_b, near, sems) = refs[9:]
    copies = [pltpu.make_async_copy(near_in.at[j], near.at[ids[j]], sems.at[j]) for j in range(near.shape[0])]
    for copy in copies:
        copy.start()
    for src, dst in (
            (one[:, 0:3 * D], qkv_a), (one[:, 3 * D:4 * D], out_a), (one[:, 4 * D:5 * D], cross_q),
            (one[:, 5 * D:7 * D], cross_kv), (one[:, 7 * D:8 * D], cross_out), (up_one[...], g_up_a), (down_one[...], g_down_a),
            (two[:, 0:3 * D], qkv_b), (two[:, 3 * D:4 * D], out_b), (up_two[...], g_up_b), (down_two[...], g_down_b)):
        dst[...] = src
    start = 0
    for ref in (gains_a, biases_a, gains_b, biases_b, bias_up_a, bias_up_b):
        ref[...] = small[start:start + ref.shape[0], :ref.shape[1]]
        start += ref.shape[0]
    for copy in copies:
        copy.wait()


def split_gradients(owned, near, near_index, D, quarter, part):
    rows = owned[2].shape[0]
    shapes = [(3, part), (10, part), (part, 3 * D), (part, D), (part, D), (part, 2 * D), (part, D), (part, quarter * D),
              (1, quarter * part), (rows, D), (2, part), (6, part), (part, 3 * D), (part, D), (part, quarter * D),
              (1, quarter * part), (rows, D), near.shape]
    vmem, hbm = pl.BlockSpec(memory_space=pltpu.VMEM), pl.BlockSpec(memory_space=pl.ANY)
    return pl.pallas_call(
        functools.partial(split_kernel, D),
        out_shape=[jax.ShapeDtypeStruct(shape, jnp.float32) for shape in shapes],
        in_specs=[vmem] * 8 + [pl.BlockSpec(memory_space=pltpu.SMEM)],
        out_specs=[vmem] * 17 + [hbm],
        scratch_shapes=[pltpu.SemaphoreType.DMA((near.shape[0],))],
        compiler_params=pltpu.CompilerParams(vmem_limit_bytes=VMEM_MOST),
        name="split_gradients",
    )(*owned, near, near_index)


F32, BF16 = jnp.float32, jnp.bfloat16
SCALE = HEAD_DIM ** (-0.5)
NN, NT = (((1,), (0,)), ((), ())), (((1,), (1,)), ((), ()))
GELU_ONE, GELU_TWO = (2.0 / 3.141592653589793) ** 0.5, 0.044715


def dot(left, right, dims=NN):
    return lax.dot_general(left, right, dims, preferred_element_type=F32)


def span_of(index, width):
    return pl.ds(pl.multiple_of(index * width, width), width)


def row_blocks(count, action, block=64):
    pl.loop(0, count // block)(lambda i: action(span_of(i, block)))


def normalise(h):
    centred = h - jnp.mean(h, axis=-1, keepdims=True)
    inverse = lax.rsqrt(jnp.mean(centred * centred, axis=-1, keepdims=True) + 1e-05)
    return centred * inverse, inverse


def fill_allowed(allowed, segments):
    shape = allowed.shape
    of_key = jnp.broadcast_to(segments[...].astype(F32), shape)
    above = lax.broadcasted_iota(jnp.int32, shape, 0) >= lax.broadcasted_iota(jnp.int32, shape, 1)
    allowed[...] = (above & (of_key.T == of_key)).astype(jnp.int32)


def norm_forward(h_ref, n_ref, gain, shift):
    def block(rows):
        xhat, _ = normalise(h_ref[rows, :].astype(F32))
        n_ref[rows, :] = (xhat * gain + shift).astype(BF16)
    row_blocks(h_ref.shape[0], block)


def norm_backward(h_ref, gain, gn_ref, g_ref, vec_ref, gain_row, shift_row):
    width = h_ref.shape[1]

    def block(i, sums):
        rows = span_of(i, 64)
        xhat, inverse = normalise(h_ref[rows, :].astype(F32))
        gn = gn_ref[rows, :]
        product = gn * xhat
        scaled = gn * gain
        inner = jnp.mean(scaled * xhat, axis=-1, keepdims=True)
        g_ref[rows, :] += inverse * (scaled - jnp.mean(scaled, axis=-1, keepdims=True) - xhat * inner)
        return sums[0] + jnp.sum(product, axis=0, keepdims=True), sums[1] + jnp.sum(gn, axis=0, keepdims=True)
    zero = jnp.zeros((1, width), F32)
    of_gain, of_shift = lax.fori_loop(0, h_ref.shape[0] // 64, block, (zero, zero))
    vec_ref[gain_row:gain_row + 1, :] = of_gain
    vec_ref[shift_row:shift_row + 1, :] = of_shift


def column_sum(values):
    return jnp.sum(values.astype(F32), axis=0, keepdims=True)


def weight_gradient(dst_ref, left_ref, right_ref, tile):
    wide = right_ref.shape[1]

    def block(i):
        rows = span_of(i, 256)
        turned = left_ref[:, rows].T
        for start in range(0, wide, tile):
            dst_ref[rows, start:start + tile] = dot(turned, right_ref[:, start:start + tile]).astype(BF16)
    pl.loop(0, left_ref.shape[1] // 256)(block)


def both_heads(pair, low_half):
    none = jnp.zeros_like(pair)
    return jnp.concatenate([jnp.where(low_half, pair, none), jnp.where(low_half, none, pair)], axis=0)


def of_both(stacked, low_half):
    rows = stacked.shape[0] // 2
    return jnp.where(low_half, stacked[:rows], stacked[rows:])


def lane_half(rows):
    return lax.broadcasted_iota(jnp.int32, (rows, 2 * HEAD_DIM), 1) < HEAD_DIM


def attend(q, k, v, seen):
    low = lane_half(q.shape[0])
    scores = jnp.where(seen, dot(both_heads(q, low), k, NT) * SCALE, -1e30)
    top = jnp.max(scores, axis=-1, keepdims=True)
    raised = jnp.exp(scores - top)
    total = jnp.sum(raised, axis=-1, keepdims=True)
    mixed = dot((raised / total).astype(BF16), v)
    return of_both(mixed, low), top + jnp.log(total)


def attend_back(q, k, v, seen, logsum, gm):
    low = lane_half(q.shape[0])
    q2, gm2 = both_heads(q, low), both_heads(gm, low)
    scores = jnp.where(seen, dot(q2, k, NT) * SCALE, -1e30)
    probs = jnp.exp(scores - logsum)
    grad_probs = dot(gm2, v, NT)
    grad_v = dot(probs.astype(BF16).T, gm2)
    inner = jnp.sum(probs * grad_probs, axis=-1, keepdims=True)
    grad_scores = (probs * (grad_probs - inner)).astype(BF16)
    grad_q = of_both(dot(grad_scores, k), low) * SCALE
    grad_k = dot(grad_scores.T, q2) * SCALE
    return grad_q, grad_k, grad_v


def gelu_both(x):
    square = x * x
    bent = jnp.tanh(GELU_ONE * x * (1.0 + GELU_TWO * square))
    half = 0.5 * (1.0 + bent)
    slope = half + 0.5 * x * (1.0 - bent * bent) * (GELU_ONE * (1.0 + 3.0 * GELU_TWO * square))
    return x * half, slope


def linear(out_ref, left_ref, w_ref, first, count, tile, bias=None):
    def block(j):
        value = dot(left_ref[...], w_ref[:, pl.ds(pl.multiple_of(first + j * tile, 128), tile)])
        if bias is not None:
            value = value + bias(j)
        out_ref[:, span_of(j, tile)] = value.astype(out_ref.dtype)
    pl.loop(0, count // tile)(block)


def self_forward(e, i, h_in, h_out, w, gain, shift, bq, bv, bo, norm):
    D = h_in.shape[1]
    n, packed, mixed, logsum = e.n.at[norm], e.packed.at[i], e.mixed.at[i], e.logsum.at[i]
    norm_forward(h_in, n, gain, shift)
    zero = jnp.zeros_like(bq)

    def bias(j):
        return jnp.where(j == 0, bq, jnp.where(j == 2, bv, zero))
    linear(packed, n, w, 0, 3 * D, D, bias)
    seen = e.allowed[...] != 0
    seen = jnp.concatenate([seen, seen], axis=0)
    for p in range(D // 128):
        a = p * 128
        value, sums = attend(packed[:, a:a + 128], packed[:, D + a:D + a + 128], packed[:, 2 * D + a:2 * D + a + 128], seen)
        mixed[:, a:a + 128] = value.astype(BF16)
        logsum[:, p:p + 1] = sums
    h_out[...] = h_in[...].astype(F32) + dot(mixed[...], w[:, 3 * D:4 * D]) + bo


def cross_pairs(e):
    neighbours, keys = e.near.shape[0], e.near.shape[1]
    spans = e.spans
    return spans, neighbours // spans * keys, e.queries.shape[0] // spans


def cross_seen(e, span):
    near = e.near.shape[0] // e.spans
    return jnp.concatenate([e.near_tokens[pl.ds(span * near + j, 1), :] for j in range(near)], axis=1) != 0


def cross_keys(e, w, bv):
    D = e.near.shape[2]
    near = e.near

    def rows(i):
        for j in range(2):
            value = dot(near[2 * i:2 * i + 2].reshape(-1, D) if isinstance(i, int) else near[pl.ds(2 * i, 2)].reshape(-1, D),
                        w[:, D + j * D:2 * D + j * D])
            if j == 1:
                value = value + bv
            e.kv[span_of(i, 2 * near.shape[1]), j * D:(j + 1) * D] = value.astype(BF16)
    pl.loop(0, near.shape[0] // 2)(rows)


def cross_forward(e, h_in, h_out, w, gain, shift, bq, bo):
    D = h_in.shape[1]
    n, queries, kv, mixed, logsum = e.n.at[1], e.queries, e.kv, e.mixed.at[2], e.logsum.at[2]
    norm_forward(h_in, n, gain, shift)
    linear(queries, n, w, 0, D, D, lambda j: bq)
    spans, keys, size = cross_pairs(e)

    def span(c):
        rows, krows = span_of(c, size), span_of(c, keys)
        seen = cross_seen(e, c)
        for p in range(D // 128):
            a = p * 128
            value, sums = attend(queries[rows, a:a + 128], kv[krows, a:a + 128], kv[krows, D + a:D + a + 128], seen)
            mixed[rows, a:a + 128] = value.astype(BF16)
            logsum[span_of(c, 2 * size), p:p + 1] = sums
    pl.loop(0, spans)(span)
    h_out[...] = h_in[...] + dot(mixed[...], w[:, 3 * D:4 * D]) + bo


def ffn_forward(e, i, h_in, w_up, w_down, gain, shift, b_up, bd, norm, write):
    D, FF = h_in.shape[1], w_up.shape[1]
    n, slope, active, total = e.n.at[norm], e.slope.at[i], e.active.at[i], e.gn
    norm_forward(h_in, n, gain, shift)

    def up(j):
        cols = span_of(j, D)
        value = dot(n[...], w_up[:, cols]) + b_up[:, cols]
        raised, bent = gelu_both(value)
        active[:, cols] = raised.astype(BF16)
        slope[:, cols] = bent
    pl.loop(0, FF // D)(up)
    total[...] = h_in[...] + bd

    def down(j):
        rows = span_of(j, D)
        total[...] += dot(active[:, rows], w_down[rows, :])
    pl.loop(0, FF // D)(down)
    write(total)


def ffn_backward(e, i, h_in, w_up, w_down, gain, norm, rows, b_row):
    D, FF = h_in.shape[1], w_up.shape[1]
    n, slope, active = e.n.at[norm], e.slope.at[i], e.active.at[i]
    g, gb, gh, gn, vec = e.g, e.gb, e.gh, e.gn, e.vec
    gb[...] = g[...].astype(BF16)
    vec[rows[2]:rows[2] + 1, :] = column_sum(gb[...])

    def hidden(j):
        cols = span_of(j, D)
        value = (dot(gb[...], w_down[cols, :], NT) * slope[:, cols].astype(F32)).astype(BF16)
        gh[:, cols] = value
        e.vec_up[i:i + 1, cols] = column_sum(value)
    pl.loop(0, FF // D)(hidden)
    gn[...] = jnp.zeros_like(gn)

    def back(j):
        cols = span_of(j, D)
        gn[...] += dot(gh[:, cols], w_up[:, cols], NT)
    pl.loop(0, FF // D)(back)
    weight_gradient(w_down, active, gb, D)
    e.ship(b_row)
    weight_gradient(w_up, n, gh, D)
    e.ship(b_row + 1)
    norm_backward(h_in, gain, gn, g, vec, rows[0], rows[1])


def self_backward(e, i, h_in, w, gain, norm, rows, ship):
    D = h_in.shape[1]
    n, packed, mixed, logsum = e.n.at[norm], e.packed.at[i], e.mixed.at[i], e.logsum.at[i]
    g, gb, gmix, gpacked, gn, vec = e.g, e.gb, e.gmix, e.gpacked, e.gn, e.vec
    gb[...] = g[...].astype(BF16)
    vec[rows[4]:rows[4] + 1, :] = column_sum(gb[...])
    gmix[...] = dot(gb[...], w[:, 3 * D:4 * D], NT).astype(BF16)
    seen = e.allowed[...] != 0
    seen = jnp.concatenate([seen, seen], axis=0)
    for p in range(D // 128):
        a = p * 128
        q, k, v = (slice(t * D + a, t * D + a + 128) for t in range(3))
        of_q, of_k, of_v = attend_back(
            packed[:, q], packed[:, k], packed[:, v], seen, logsum[:, p:p + 1], gmix[:, a:a + 128])
        gpacked[:, q], gpacked[:, k], gpacked[:, v] = of_q.astype(BF16), of_k.astype(BF16), of_v.astype(BF16)
    vec[rows[2]:rows[2] + 1, :] = column_sum(gpacked[:, :D])
    vec[rows[3]:rows[3] + 1, :] = column_sum(gpacked[:, 2 * D:])
    gn[...] = jnp.zeros_like(gn)

    def back(j):
        cols = span_of(j, D)
        gn[...] += dot(gpacked[:, cols], w[:, cols], NT)
    pl.loop(0, 3)(back)
    weight_gradient(w.at[:, 0:3 * D], n, gpacked, D)
    weight_gradient(w.at[:, 3 * D:4 * D], mixed, gb, D)
    e.ship(ship)
    norm_backward(h_in, gain, gn, g, vec, rows[0], rows[1])


def cross_backward(e, h_in, w, gain, rows, ship):
    D = h_in.shape[1]
    n, queries, kv, mixed, logsum = e.n.at[1], e.queries, e.kv, e.mixed.at[2], e.logsum.at[2]
    g, gb, gmix, gq, gkv, gn, vec = e.g, e.gb, e.gmix, e.gpacked, e.gkv, e.gn, e.vec
    near = e.near
    gb[...] = g[...].astype(BF16)
    vec[rows[4]:rows[4] + 1, :] = column_sum(gb[...])
    gmix[...] = dot(gb[...], w[:, 3 * D:4 * D], NT).astype(BF16)
    spans, keys, size = cross_pairs(e)

    def span(c):
        srows, krows = span_of(c, size), span_of(c, keys)
        seen = cross_seen(e, c)
        for p in range(D // 128):
            a, b = p * 128, D + p * 128
            of_q, of_k, of_v = attend_back(
                queries[srows, a:a + 128], kv[krows, a:a + 128], kv[krows, b:b + 128], seen,
                logsum[span_of(c, 2 * size), p:p + 1], gmix[srows, a:a + 128])
            gq[srows, a:a + 128] = of_q.astype(BF16)
            gkv[krows, a:a + 128], gkv[krows, b:b + 128] = of_k.astype(BF16), of_v.astype(BF16)
    pl.loop(0, spans)(span)
    vec[rows[2]:rows[2] + 1, :] = column_sum(gq[:, :D])
    vec[rows[3]:rows[3] + 1, :] = column_sum(gkv[:, D:])
    gn[...] = dot(gq[:, :D], w[:, 0:D], NT)
    length = near.shape[1]

    def near_rows(i):
        krows = span_of(i, 2 * length)
        value = dot(gkv[krows, :D], w[:, D:2 * D], NT) + dot(gkv[krows, D:], w[:, 2 * D:3 * D], NT)
        e.near_out(i, value.reshape(2, length, D))
    pl.loop(0, near.shape[0] // 2)(near_rows)
    weight_gradient(w.at[:, 0:D], n, gq.at[:, 0:D], D)

    def pair(i):
        cols = span_of(i, 256)
        turned = near[:, :, cols].reshape(-1, 256).T
        for j in range(2):
            w[cols, D + j * D:2 * D + j * D] = dot(turned, gkv[:, j * D:(j + 1) * D]).astype(BF16)
    pl.loop(0, D // 256)(pair)
    weight_gradient(w.at[:, 3 * D:4 * D], mixed, gb, D)
    e.ship(ship)
    norm_backward(h_in, gain, gn, g, vec, rows[0], rows[1])


def block_kernel(spans, *refs):
    (ids, tokens, cotangent, segments, neighbours, stored_tokens, rows, bias_up,
     first, up_a, down_a, second, up_b, down_b,
     out, grad_tokens, grad_near, g_first, g_up_a, g_down_a, g_second, g_up_b, g_down_b, vec, vec_up,
     h, n, packed, mixed, logsum, queries, kv, near, near_tokens, slope, active, allowed,
     gb, gmix, gpacked, gkv, gh, gn, wide, tall, near_stage, loads, ships, nears, near_sems) = refs
    D = tokens.shape[1]
    FF = 4 * D

    def load(number):
        src, dst = (
            (first.at[:, 0:FF], wide.at[0]), (first.at[:, FF:2 * FF], wide.at[1]), (up_a, wide.at[2]), (down_a, tall.at[0]),
            (second, wide.at[0]), (up_b, wide.at[1]), (down_b, tall.at[1]),
            (first.at[:, FF:2 * FF], wide.at[1]), (first.at[:, 0:FF], wide.at[0]))[number]
        return pltpu.make_async_copy(src, dst, loads.at[number])

    def ship_copy(number):
        src, dst = (
            (tall.at[1], g_down_b), (wide.at[1], g_up_b), (wide.at[0], g_second), (tall.at[0], g_down_a),
            (wide.at[2], g_up_a), (wide.at[1], g_first.at[:, FF:2 * FF]), (wide.at[0], g_first.at[:, 0:FF]))[number]
        return pltpu.make_async_copy(src, dst, ships.at[number])

    def near_copy(j):
        return pltpu.make_async_copy(neighbours.at[ids[j]], near.at[j], nears.at[j])

    count = near.shape[0]
    for number in (0, 1, 2, 3, 6):
        load(number).start()
    for j in range(count):
        near_copy(j).start()
    for j in range(count):
        near_tokens[j:j + 1, :] = stored_tokens[pl.ds(ids[j], 1), :]
    grad_near_stage = near_stage

    def near_write(i, half):
        return pltpu.make_async_copy(grad_near_stage.at[i % 2, half], grad_near.at[ids[2 * i + half]], near_sems.at[i % 2, half])

    def near_out(i, value):
        @pl.when(i >= 2)
        def _():
            for half in range(2):
                near_write(i, half).wait()
        grad_near_stage[i % 2] = value
        for half in range(2):
            near_write(i, half).start()

    fill_allowed(allowed, segments)
    e = types.SimpleNamespace(n=n, packed=packed, mixed=mixed, logsum=logsum, queries=queries, kv=kv, near=near, near_tokens=near_tokens,
             slope=slope, active=active, allowed=allowed, g=grad_tokens, gb=gb, gmix=gmix, gpacked=gpacked, gkv=gkv, gh=gh,
             gn=gn, vec=vec, vec_up=vec_up, spans=spans, ship=lambda number: ship_copy(number).start(), near_out=near_out)

    def row(i):
        return rows[i:i + 1, :]
    load(0).wait()
    self_forward(e, 0, tokens, h.at[0], wide.at[0], row(0), row(3), row(6), row(7), row(8), 0)
    load(4).start()
    load(1).wait()
    for j in range(count):
        near_copy(j).wait()
    cross_keys(e, wide.at[1], row(10))
    cross_forward(e, h.at[0], h.at[1], wide.at[1], row(1), row(4), row(9), row(11))
    load(5).start()
    load(2).wait()
    load(3).wait()

    def keep(total):
        h[2] = total[...]
    ffn_forward(e, 0, h.at[1], wide.at[2], tall.at[0], row(2), row(5), bias_up.at[0:1], row(12), 2, keep)
    load(4).wait()
    self_forward(e, 1, h.at[2], h.at[3], wide.at[0], row(13), row(15), row(17), row(18), row(19), 3)
    load(5).wait()
    load(6).wait()

    def finish(total):
        out[...] = total[...].astype(BF16)
    ffn_forward(e, 1, h.at[3], wide.at[1], tall.at[1], row(14), row(16), bias_up.at[1:2], row(20), 4, finish)
    grad_tokens[...] = cotangent[...].astype(F32)
    ffn_backward(e, 1, h.at[3], wide.at[1], tall.at[1], row(14), 4, (14, 16, 20), 0)
    ship_copy(1).wait()
    load(7).start()
    self_backward(e, 1, h.at[2], wide.at[0], row(13), 3, (13, 15, 17, 18, 19), 2)
    ship_copy(2).wait()
    load(8).start()
    ffn_backward(e, 0, h.at[1], wide.at[2], tall.at[0], row(2), 2, (2, 5, 12), 3)
    load(7).wait()
    cross_backward(e, h.at[0], wide.at[1], row(1), (1, 4, 9, 10, 11), 5)
    load(8).wait()
    self_backward(e, 0, tokens, wide.at[0], row(0), 0, (0, 3, 6, 7, 8), 6)
    for number in (0, 3, 4, 5, 6):
        ship_copy(number).wait()
    for i in (count // 2 - 2, count // 2 - 1):
        for half in range(2):
            near_write(i, half).wait()


def run_blocks(tokens, cotangent, segment_ids, neighbours, near_index, neighbour_tokens, spans, rows, bias_up, weights):
    T, D = tokens.shape
    FF = 4 * D
    count, length, _ = neighbours.shape
    vmem, hbm = pl.BlockSpec(memory_space=pltpu.VMEM), pl.BlockSpec(memory_space=pl.ANY)
    shape = jax.ShapeDtypeStruct
    return pl.pallas_call(
        functools.partial(block_kernel, spans),
        out_shape=[shape((T, D), BF16), shape((T, D), F32), shape(neighbours.shape, F32)]
        + [shape(w.shape, BF16) for w in weights] + [shape((24, D), F32), shape((8, FF), F32)],
        in_specs=[pl.BlockSpec(memory_space=pltpu.SMEM), vmem, vmem, vmem, hbm, vmem, vmem, vmem] + [hbm] * 6,
        out_specs=[vmem, vmem, hbm] + [hbm] * 6 + [vmem, vmem],
        scratch_shapes=[
            pltpu.VMEM((4, T, D), F32), pltpu.VMEM((5, T, D), BF16), pltpu.VMEM((2, T, 3 * D), BF16),
            pltpu.VMEM((3, T, D), BF16), pltpu.VMEM((3, 2 * T, 128), F32), pltpu.VMEM((T, D), BF16),
            pltpu.VMEM((count * length, 2 * D), BF16), pltpu.VMEM(neighbours.shape, BF16),
            pltpu.VMEM((count, length), jnp.int32), pltpu.VMEM((2, T, FF), F32), pltpu.VMEM((2, T, FF), BF16),
            pltpu.VMEM((T, T), jnp.int32), pltpu.VMEM((T, D), BF16), pltpu.VMEM((T, D), BF16),
            pltpu.VMEM((T, 3 * D), BF16), pltpu.VMEM((count * length, 2 * D), BF16), pltpu.VMEM((T, FF), BF16),
            pltpu.VMEM((T, D), F32), pltpu.VMEM((3, D, FF), BF16), pltpu.VMEM((2, FF, D), BF16),
            pltpu.VMEM((2, 2, length, D), F32),
            pltpu.SemaphoreType.DMA((9,)), pltpu.SemaphoreType.DMA((7,)), pltpu.SemaphoreType.DMA((count,)),
            pltpu.SemaphoreType.DMA((2, 2)),
        ],
        compiler_params=pltpu.CompilerParams(vmem_limit_bytes=63 * 2 ** 20, has_side_effects=True),
        name="blocks",
    )(near_index, tokens, cotangent, segment_ids, neighbours, neighbour_tokens, rows, bias_up,
      *weights)


def parameter_tile(ref, start, width):
    tile = ref[(slice(None),) * 5 + (pl.ds(start, width),)]
    rows = math.prod(tile.shape[:5])
    if tile.shape[4] % 16:
        return tile.astype(F32).reshape(rows, width).astype(BF16)
    return tile.reshape(rows, width)


def project(out_ref, out_col, lefts, w_ref, w_col, count, bias=None, action=None):
    tile = 256

    def block(j):
        for start in range(0, group, tile):
            here = j * group + start
            weights = parameter_tile(w_ref, pl.multiple_of(w_col + here, tile), tile)
            cols = pl.ds(pl.multiple_of(out_col + here, tile), tile)
            row = 0
            for left in lefts():
                value = dot(left, weights)
                if bias is not None:
                    value = value + bias[:, pl.ds(pl.multiple_of(here, tile), tile)]
                if action is not None:
                    action(cols, value)
                else:
                    out_ref[row:row + left.shape[0], cols] = value.astype(out_ref.dtype)
                row += left.shape[0]
    group = 3 * tile if count % (3 * tile) == 0 else tile
    pl.loop(0, count // group)(block)


def self_pieces(e, i, norm, h_in, h_out, w, chunk, gain, bias_rows):
    D = h_in.shape[1]
    n, packed, mixed, logsum, rows = e.n, e.packed, e.mixed, e.logsum, e.rows
    shift, bq, bv, bo = bias_rows

    def bias(row):
        return rows.at[row:row + 1, :]
    yield chunk, 3.0
    e.free("n")
    norm_forward(h_in, n, rows[gain:gain + 1, :], rows[shift:shift + 1, :])
    e.save("n", norm)
    e.free("packed")
    project(packed, 0, lambda: [n[...]], w, 0, D, bias(bq))
    project(packed, D, lambda: [n[...]], w, D, D)
    yield chunk + 1, 1.0
    project(packed, 2 * D, lambda: [n[...]], w, 2 * D, D, bias(bv))
    e.save("packed", i)
    e.free("mixed")
    e.free("logsum")
    for p in range(D // 128):
        if p % 3 == 0:
            yield chunk + 1, 2.0
        seen = e.allowed[...] != 0
        seen = jnp.concatenate([seen, seen], axis=0)
        a = p * 128
        value, sums = attend(packed[:, a:a + 128], packed[:, D + a:D + a + 128], packed[:, 2 * D + a:2 * D + a + 128], seen)
        mixed[:, a:a + 128] = value.astype(BF16)
        logsum[:, p:p + 1] = sums
    e.save("mixed", i)
    e.save("logsum", i)
    yield chunk + 1, 1.0

    def add(cols, value):
        h_out[:, cols] = h_in[:, cols].astype(F32) + value
    project(None, 0, lambda: [mixed[...]], w, 3 * D, D, bias(bo), add)
    e.save("h", 3 * i)


def cross_pieces(e, norm, h_in, h_out, w, chunk, gain, bias_rows):
    D = h_in.shape[1]
    n, queries, kv, mixed, logsum, rows = e.n, e.queries, e.kv, e.mixed, e.logsum, e.rows
    near, near_tokens, spans = e.near, e.near_tokens, e.spans
    count, length = near.shape[0], near.shape[1]
    shift, bq, bv, bo = bias_rows
    yield chunk, 2.0
    e.free("n")
    norm_forward(h_in, n, rows[gain:gain + 1, :], rows[shift:shift + 1, :])
    e.save("n", norm)
    project(queries, 0, lambda: [n[...]], w, 4 * D, D, rows.at[bq:bq + 1, :])
    e.save("queries", 0)
    flat = lambda: [near[j:j + 2].reshape(2 * length, D) for j in range(0, count, 2)]
    yield chunk, 3.0
    project(kv, 0, flat, w, 5 * D, D)
    yield chunk + 1, 3.0
    project(kv, D, flat, w, 6 * D, D, rows.at[bv:bv + 1, :])
    e.save("kv", 0)
    e.free("mixed")
    e.free("logsum")
    size, each = n.shape[0] // spans, count // spans
    for c in range(spans):
        yield chunk + 1, 1.3
        seen = jnp.concatenate([near_tokens[c * each + j:c * each + j + 1, :] for j in range(each)], axis=1) != 0

        def read(col):
            return kv[c * each * length:(c + 1) * each * length, col:col + 128]
        for p in range(D // 128):
            a = p * 128
            value, sums = attend(queries[c * size:(c + 1) * size, a:a + 128], read(a), read(D + a), seen)
            mixed[c * size:(c + 1) * size, a:a + 128] = value.astype(BF16)
            logsum[2 * c * size:2 * (c + 1) * size, p:p + 1] = sums
    e.save("mixed", 2)
    e.save("logsum", 2)
    yield chunk + 1, 1.0

    def add(cols, value):
        h_out[:, cols] = h_in[:, cols] + value
    project(None, 0, lambda: [mixed[...]], w, 7 * D, D, rows.at[bo:bo + 1, :], add)
    e.save("h", 1)


def ffn_pieces(e, i, norm, h_in, w_up, w_down, chunk, gain, bias_rows, finish):
    D = h_in.shape[1]
    n, slope, active, rows, total = e.n, e.slope, e.active, e.rows, e.total
    shift, bd = bias_rows
    FF = active.shape[1]
    yield chunk, 1.0
    e.free("n")
    norm_forward(h_in, n, rows[gain:gain + 1, :], rows[shift:shift + 1, :])
    e.save("n", norm)
    e.free("slope")
    e.free("active")

    def action(cols, value):
        raised, bent = gelu_both(value)
        active[:, cols] = raised.astype(BF16)
        slope[:, cols] = bent.astype(BF16)
    for j in range(FF // D):
        yield chunk + (2 * j * D) // FF, 1.3
        project(None, j * D, lambda: [n[...]], w_up, j * D, D, e.bias_up.at[i:i + 1, j * D:(j + 1) * D], action)
    e.save("slope", i)
    e.save("active", i)

    def add(cols, value):
        total[:, cols] = h_in[:, cols] + value
    yield chunk + 3, 3.0
    project(None, 0, lambda: [active[...]], w_down, 0, D, rows.at[bd:bd + 1, :], add)
    finish()


def forward_pieces(e, h, tokens, first, up_a, down_a, second, up_b, down_b, small):
    yield 0, 1.5
    lines = [small[index] for index in itertools.product(*map(range, small.shape[:4]))]
    part = e.rows.shape[1] // len(lines)
    wide = e.bias_up.shape[1] // len(lines)
    e.rows[...] = jnp.concatenate([line[:24, :part].astype(F32) for line in lines], axis=1)
    both = jnp.concatenate([line[16:24, :wide].astype(F32) for line in lines], axis=1)
    e.bias_up[...] = both[5:7]
    yield from self_pieces(e, 0, 0, tokens, h.at[0], first, 0, 0, (3, 6, 7, 8))
    yield from cross_pieces(e, 1, h.at[0], h.at[1], first, 2, 1, (4, 9, 10, 11))

    def keep():
        h[2] = e.total[...]
        e.save("h", 2)
    yield from ffn_pieces(e, 0, 2, h.at[1], up_a, down_a, 4, 2, (5, 12), keep)
    yield from self_pieces(e, 1, 3, h.at[2], h.at[3], second, 8, 13, (15, 17, 18, 19))

    def finish():
        e.out[...] = e.total[...].astype(BF16)
    yield from ffn_pieces(e, 1, 4, h.at[3], up_b, down_b, 10, 14, (16, 20), finish)


SAVED = ("n", "packed", "queries", "kv", "mixed", "logsum", "slope", "active")


def forward_kernel(dp_size, fsdp_size, chunks, places, count, spans, *refs):
    n = len(places)
    shards, vectors, (tokens, segments, near, near_tokens) = refs[:n], refs[n:n + 6], refs[n + 6:n + 10]
    refs = refs[n + 10:]
    wholes, (out, h_out, rows), saved = refs[:count - 1], refs[count - 1:count + 2], dict(zip(SAVED, refs[count + 2:count + 10]))
    refs = refs[count + 10:]
    landing, held, (h, allowed, total, bias_up) = refs[:count], dict(zip(SAVED, refs[count:count + 8])), refs[count + 8:count + 12]
    kept, saves, send, recv = refs[count + 12:]
    place = Place(dp_size, fsdp_size)
    here = tuple(place.at[name] for name in NAMES)
    for shard, (which, col) in zip(shards, places):
        landing[which][(*here, slice(None), slice(col, col + shard.shape[1]))] = shard[...]
    landing[count - 1][here] = pack_small(vectors[:4], vectors[4:])
    greet(place)
    sems = Sems(send, recv)
    copies, pending, used = [], {}, [0]

    def keep(slot, which, row, height, col, width):
        where = (slice(None),) * 4 + (pl.ds(row, height), pl.ds(col, width))
        copy = pltpu.make_async_copy(landing[which].at[where], wholes[which].at[where], kept.at[slot])
        copy.start()
        copies.append(copy)

    def chunk_flow(slots, group):
        flows = [
            gather_flow(place, sems, landing[which], order, row, height, start + col, width)
            for which, row, height, start, total in group
            for order, col, width in routes(total)
        ]
        while flows:
            flows = [flow for flow in flows if next(flow, 0) is None]
            if flows:
                yield
        for slot, member in zip(slots, group):
            if member[0] < count - 1:
                keep(slot, *member)

    def save(name, index):
        src, dst = (h.at[index], h_out.at[index]) if name == "h" else (held[name], saved[name].at[index])
        copy = pltpu.make_async_copy(src, dst, saves.at[used[0]])
        copy.start()
        used[0] += 1
        pending[(name, index) if name == "h" else name] = copy

    def free(name):
        if name in pending:
            pending.pop(name).wait()

    fill_allowed(allowed, segments)
    e = types.SimpleNamespace(**held, rows=rows, bias_up=bias_up, allowed=allowed, near=near, near_tokens=near_tokens, spans=spans,
             total=total, out=out, save=save, free=free)
    work = forward_pieces(e, h, tokens, *landing)
    ahead = next(work, None)
    groups, slot = [], 0
    for group in chunks:
        groups.append([chunk_flow(range(slot, slot + len(group)), group)])
        slot += len(group)

    def compute(tick, ahead=[ahead]):
        left = COMPUTE_SHARE
        last = tick == len(groups) + GATHER_STEPS[-1] - 1
        while ahead[0] is not None and ahead[0][0] + GATHER_STEPS[-1] <= tick and (left > 0 or last):
            left -= ahead[0][1]
            ahead[0] = next(work, None)
    run_schedule(groups, GATHER_STEPS, compute)
    sems.drain()
    for copy in copies + list(pending.values()):
        copy.wait()


def arrange_kernel(ids, neighbours, stored_tokens, near, near_tokens, sems):
    copies = [pltpu.make_async_copy(neighbours.at[ids[j]], near.at[j], sems.at[j]) for j in range(near.shape[0])]
    for copy in copies:
        copy.start()
    for j in range(near.shape[0]):
        near_tokens[j:j + 1, :] = stored_tokens[pl.ds(ids[j], 1), :]
    for copy in copies:
        copy.wait()


def arrange(near_index, neighbours, neighbour_tokens):
    vmem, hbm = pl.BlockSpec(memory_space=pltpu.VMEM), pl.BlockSpec(memory_space=pl.ANY)
    return pl.pallas_call(
        arrange_kernel,
        out_shape=[jax.ShapeDtypeStruct(x.shape, x.dtype) for x in (neighbours, neighbour_tokens)],
        in_specs=[pl.BlockSpec(memory_space=pltpu.SMEM), hbm, vmem],
        out_specs=[vmem, vmem],
        scratch_shapes=[pltpu.SemaphoreType.DMA((neighbours.shape[0],))],
        name="arrange_neighbours",
    )(near_index, neighbours, neighbour_tokens)


def gather_and_run(mesh_shape, shards, places, vectors, chunks, tokens, segment_ids, neighbours, neighbour_tokens,
                   spans, collective_id):
    dp_size, fsdp_size = mesh_shape
    size = {"y": dp_size // 2, "c": 2, "z": fsdp_size // 2, "x": 2}
    count = sum(copies_of(order, size) for group in chunks for *_, total in group for order, _, _ in routes(total))
    count += sum(1 for group in chunks for *_, total in group for _ in routes(total))
    lead = tuple(size[name] for name in NAMES)
    shapes = {}
    for shard, (which, col) in zip(shards, places):
        rows, width = shapes.get(which, (shard.shape[0], 0))
        shapes[which] = (rows, max(width, col + shard.shape[1]))
    shapes = [shapes[which] for which in sorted(shapes)] + [(32, 128)]
    T, D = tokens.shape
    FF = 4 * D
    near, length, _ = neighbours.shape
    shape = jax.ShapeDtypeStruct
    held = {"n": ((T, D), BF16, 5), "packed": ((T, 3 * D), BF16, 2), "queries": ((T, D), BF16, 1),
            "kv": ((near * length, 2 * D), BF16, 1), "mixed": ((T, D), BF16, 3), "logsum": ((2 * T, 128), F32, 3),
            "slope": ((T, FF), BF16, 2), "active": ((T, FF), BF16, 2)}
    n, vmem, hbm = len(shards), pl.BlockSpec(memory_space=pltpu.VMEM), pl.BlockSpec(memory_space=pl.ANY)
    results = pl.pallas_call(
        functools.partial(forward_kernel, dp_size, fsdp_size, chunks, places, len(shapes), spans),
        out_shape=[shape(lead + s, BF16) for s in shapes[:-1]]
        + [shape((T, D), BF16), shape((4, T, D), F32), shape((24, D), F32)]
        + [shape((times,) + s, kind) for s, kind, times in held.values()],
        in_specs=[vmem] * (n + 10),
        out_specs=[hbm] * (len(shapes) - 1) + [vmem, hbm, vmem] + [hbm] * 8,
        scratch_shapes=[pltpu.VMEM(lead + s, BF16) for s in shapes]
        + [pltpu.VMEM(s, kind) for s, kind, _ in held.values()]
        + [pltpu.VMEM((4, T, D), F32), pltpu.VMEM((T, T), jnp.int32), pltpu.VMEM((T, D), F32), pltpu.VMEM((2, FF), F32)]
        + [
            pltpu.SemaphoreType.DMA((sum(map(len, chunks)),)),
            pltpu.SemaphoreType.DMA((24,)),
            pltpu.SemaphoreType.DMA((count,)),
            pltpu.SemaphoreType.DMA((count,)),
        ],
        compiler_params=pltpu.CompilerParams(
            collective_id=collective_id, has_side_effects=True, vmem_limit_bytes=63 * 2 ** 20),
        name="gather_and_forward",
    )(*shards, *vectors, tokens, segment_ids, neighbours, neighbour_tokens)
    return results[:len(shapes) - 1], results[len(shapes) - 1:len(shapes) + 2], dict(zip(SAVED, results[len(shapes) + 2:]))


def ffn_chain(e, i, h_in, w_up, w_down, gain, norm, rows):
    D, FF = h_in.shape[1], w_up.shape[1]
    slope, gb, gh, g, gn, vec = e.slope.at[i], e.gb.at[norm], e.gh.at[i], e.g, e.gn, e.vec
    gb[...] = g[...].astype(BF16)
    vec[rows[2]:rows[2] + 1, :] = column_sum(gb[...])
    gn[...] = jnp.zeros_like(gn)

    def hidden(j):
        cols = span_of(j, D)
        value = (dot(gb[...], w_down[cols, :], NT) * slope[:, cols].astype(F32)).astype(BF16)
        gh[:, cols] = value
        e.vec_up[i:i + 1, cols] = column_sum(value)
        gn[...] += dot(value, w_up[:, cols], NT)
    pl.loop(0, FF // D)(hidden)
    e.save("gb", norm)
    e.save("gh", i)
    norm_backward(h_in, gain, gn, g, vec, rows[0], rows[1])


def self_chain(e, i, h_in, w, gain, norm, rows):
    D = h_in.shape[1]
    packed, logsum, gb, gpacked = e.packed.at[i], e.logsum.at[i], e.gb.at[norm], e.gpacked.at[i]
    g, gmix, gn, vec = e.g, e.gmix, e.gn, e.vec
    gb[...] = g[...].astype(BF16)
    vec[rows[4]:rows[4] + 1, :] = column_sum(gb[...])
    e.save("gb", norm)
    gmix[...] = dot(gb[...], w[:, 3 * D:4 * D], NT).astype(BF16)
    seen = e.allowed[...] != 0
    seen = jnp.concatenate([seen, seen], axis=0)
    for p in range(D // 128):
        a = p * 128
        q, k, v = (slice(t * D + a, t * D + a + 128) for t in range(3))
        of_q, of_k, of_v = attend_back(
            packed[:, q], packed[:, k], packed[:, v], seen, logsum[:, p:p + 1], gmix[:, a:a + 128])
        gpacked[:, q], gpacked[:, k], gpacked[:, v] = of_q.astype(BF16), of_k.astype(BF16), of_v.astype(BF16)
    e.save("gpacked", i)
    vec[rows[2]:rows[2] + 1, :] = column_sum(gpacked[:, :D])
    vec[rows[3]:rows[3] + 1, :] = column_sum(gpacked[:, 2 * D:])
    gn[...] = jnp.zeros_like(gn)

    def back(j):
        cols = span_of(j, D)
        gn[...] += dot(gpacked[:, cols], w[:, cols], NT)
    pl.loop(0, 3)(back)
    norm_backward(h_in, gain, gn, g, vec, rows[0], rows[1])


KEPT = ("packed", "logsum", "slope")
MADE = ("gb", "gh", "gpacked")


def backward_kernel(*refs):
    (cotangent, segments, rows, h_in, up_a, down_a, second, up_b, down_b) = refs[:9]
    stored = dict(zip(KEPT, refs[9:12]))
    g, vec, vec_up = refs[12:15]
    given, held, made = dict(zip(MADE, refs[15:18])), dict(zip(KEPT, refs[18:21])), dict(zip(MADE, refs[21:24]))
    (h, allowed, gmix, gn, wide, tall, loads, brought, saves) = refs[24:]

    def load(number):
        src, dst = (
            (down_b, tall.at[1]), (up_b, wide.at[1]), (second, wide.at[0]), (down_a, tall.at[0]), (up_a, wide.at[2]))[number]
        return pltpu.make_async_copy(src, dst, loads.at[number])

    wanted = ((2, 1), (3, 3), (0, 1), (1, 1), (3, 2), (2, 0), (3, 1))

    def bring(number):
        which, index = wanted[number]
        src, dst = (h_in, h) if which == 3 else (stored[KEPT[which]], held[KEPT[which]])
        return pltpu.make_async_copy(src.at[index], dst.at[index], brought.at[number])

    saved = []

    def save(name, index):
        copy = pltpu.make_async_copy(made[name].at[index], given[name].at[index], saves.at[len(saved)])
        copy.start()
        saved.append(copy)

    load(0).start()
    bring(0).start()
    load(1).start()
    bring(1).start()
    load(2).start()
    for number in range(2, len(wanted)):
        bring(number).start()
    load(3).start()
    load(4).start()
    fill_allowed(allowed, segments)
    e = types.SimpleNamespace(**held, **made, allowed=allowed, g=g, gmix=gmix, gn=gn, vec=vec, vec_up=vec_up, save=save)

    def row(i):
        return rows[i:i + 1, :]

    def ready(*numbers):
        for number in numbers:
            bring(number).wait()
    g[...] = cotangent[...].astype(F32)
    load(0).wait()
    load(1).wait()
    ready(0, 1)
    ffn_chain(e, 1, h.at[3], wide.at[1], tall.at[1], row(14), 4, (14, 16, 20))
    load(2).wait()
    ready(2, 3, 4)
    self_chain(e, 1, h.at[2], wide.at[0], row(13), 3, (13, 15, 17, 18, 19))
    load(3).wait()
    load(4).wait()
    ready(5, 6)
    ffn_chain(e, 0, h.at[1], wide.at[2], tall.at[0], row(2), 2, (2, 5, 12))
    for copy in saved:
        copy.wait()


def run_backward(cotangent, segment_ids, rows, h, saved, weights):
    T, D = cotangent.shape
    FF = 4 * D
    vmem, hbm = pl.BlockSpec(memory_space=pltpu.VMEM), pl.BlockSpec(memory_space=pl.ANY)
    shape = jax.ShapeDtypeStruct
    made = ((5, T, D), (2, T, FF), (2, T, 3 * D))
    results = pl.pallas_call(
        backward_kernel,
        out_shape=[shape((T, D), F32), shape((24, D), F32), shape((8, FF), F32)] + [shape(s, BF16) for s in made],
        in_specs=[vmem] * 3 + [hbm] * 9,
        out_specs=[vmem] * 3 + [hbm] * 3,
        scratch_shapes=[pltpu.VMEM(saved[name].shape, saved[name].dtype) for name in KEPT]
        + [pltpu.VMEM(s, BF16) for s in made] + [
            pltpu.VMEM((4, T, D), F32), pltpu.VMEM((T, T), jnp.int32), pltpu.VMEM((T, D), BF16),
            pltpu.VMEM((T, D), F32), pltpu.VMEM((3, D, FF), BF16), pltpu.VMEM((2, FF, D), BF16),
            pltpu.SemaphoreType.DMA((5,)), pltpu.SemaphoreType.DMA((7,)), pltpu.SemaphoreType.DMA((6,)),
        ],
        compiler_params=pltpu.CompilerParams(vmem_limit_bytes=VMEM_MOST, has_side_effects=True),
        name="backward",
    )(cotangent, segment_ids, rows, h, *weights, *[saved[name] for name in KEPT])
    return results[:3], dict(zip(MADE, results[3:]))


def gradient_columns(dst, j, left, right, right_col):
    size = dst.shape
    rows = math.prod(size[1:4]) * size[5]

    def block(y):
        turned = left(pl.ds(pl.multiple_of(y * rows, 128), rows)).T
        for start in range(0, size[6], 256):
            value = dot(turned, right[:, right_col + start:right_col + start + 256])
            dst[y, :, :, :, j, :, start:start + 256] = value.reshape(size[1:4] + (size[5], 256)).astype(BF16)
    pl.loop(0, size[0])(block)


def gradient_rows(dsts, left, right):
    Y, C, Z, X, parts, rows, width = dsts[0].shape
    each = 2 * X * rows * parts * len(dsts)

    def block(i):
        y, c, z = i // (C * Z // 2), (i // (Z // 2)) % C, i % (Z // 2)
        turned = left[:, pl.ds(pl.multiple_of(i * each, 128), each)].T
        for start in range(0, width, 256):
            value = dot(turned, right[:, start:start + 256]).reshape(2, X, len(dsts), parts, rows, 256).astype(BF16)
            for half, dst in enumerate(dsts):
                dst[y, c, pl.ds(2 * z, 2), :, :, :, start:start + 256] = value[:, :, half]
    pl.loop(0, left.shape[1] // each)(block)


FACTORS = ("n", "active", "mixed", "gb", "gh", "gpacked", "packed", "logsum", "kv", "queries", "h")
ORDER = (("active", 1, 0), ("gb", 4, 4), ("n", 4, 4), ("gh", 1, 0), ("kv", 0, 0), ("queries", 0, 0), ("logsum", 2, 2), ("h", 0, 0),
         ("n", 3, 3), ("gpacked", 1, 0), ("mixed", 1, 1), ("gb", 3, 3), ("packed", 0, 0), ("logsum", 0, 0), ("gb", 2, 2),
         ("n", 2, 2), ("n", 1, 1), ("mixed", 2, 2), ("n", 0, 0), ("mixed", 0, 0))
LATER = (("active", 0, 0), ("gh", 0, 0))


def chunk_makers(f, need, later, require):
    near = f.near
    D = near.shape[2]

    def rows_of(i, norm):
        def make(dsts):
            need(("active", i), ("gb", norm))
            gradient_rows(dsts, f.active.at[0], f.gb.at[norm])
            if i:
                later(0)
        return make

    def columns(dst, j, name, index, right, right_col):
        left = getattr(f, name)
        gradient_columns(dst, j, lambda rows: left[index, :, rows], right, right_col)

    def up(i, norm, half):
        def make(dsts):
            need(("n", norm), ("gh", i))
            for j in range(2):
                columns(dsts[0], j, "n", norm, f.gh.at[0], (2 * half + j) * D)
            if i and not half:
                later(1)
        return make

    def query_key(i, norm):
        def make(dsts):
            require(2 - 2 * i)
            need(("n", norm), ("gpacked", i))
            for j in range(2):
                columns(dsts[0], j, "n", norm, f.gpacked.at[0], j * D)
        return make

    def value_out(i, norm):
        def make(dsts):
            require(2 - 2 * i)
            need(("n", norm), ("gpacked", i), ("mixed", i), ("gb", norm))
            columns(dsts[0], 0, "n", norm, f.gpacked.at[0], 2 * D)
            columns(dsts[0], 1, "mixed", i, f.gb.at[norm], 0)
        return make

    def near_rows(rows):
        return near[:, :, rows].reshape(-1, rows.size)

    def cross_one(dsts):
        require(1)
        need(("n", 1))
        columns(dsts[0], 0, "n", 1, f.gq, 0)
        gradient_columns(dsts[0], 1, near_rows, f.gkv, 0)

    def cross_two(dsts):
        require(1)
        need(("mixed", 2))
        gradient_columns(dsts[0], 0, near_rows, f.gkv, D)
        columns(dsts[0], 1, "mixed", 2, f.gb.at[1], 0)
    return (rows_of(1, 4), None, up(1, 4, 1), up(1, 4, 0), value_out(1, 3), query_key(1, 3), rows_of(0, 2), None,
            up(0, 2, 1), up(0, 2, 0), cross_two, cross_one, value_out(0, 0), query_key(0, 0))


def chain_pieces(f, need, near_out, spans):
    g, gn, gmix, vec, rows, gq, gkv, gpacked = f.g, f.gn, f.gmix, f.vec, f.rows, f.gq, f.gkv, f.gpacked.at[0]
    D = g.shape[1]
    tiles = f.tiles
    yield 1.5
    need(("tiles", 0))
    gb = f.gb.at[1]
    gb[...] = g[...].astype(BF16)
    vec[11:12, :] = column_sum(gb[...])
    gmix[...] = dot(gb[...], tiles[3], NT).astype(BF16)
    near, length = f.near_tokens.shape
    each = near // spans
    keys, size = each * length, g.shape[0] // spans
    need(("kv", 0), ("queries", 0), ("logsum", 2), ("h", 0))
    queries, kv, logsum = f.queries.at[0], f.kv.at[0], f.logsum.at[2]
    for c in range(spans):
        yield 2.5
        srows, krows = slice(c * size, (c + 1) * size), slice(c * keys, (c + 1) * keys)
        seen = jnp.concatenate([f.near_tokens[c * each + j:c * each + j + 1, :] for j in range(each)], axis=1) != 0
        for p in range(D // 128):
            a, b = p * 128, D + p * 128
            of_q, of_k, of_v = attend_back(
                queries[srows, a:a + 128], kv[krows, a:a + 128], kv[krows, b:b + 128], seen,
                logsum[2 * c * size:2 * (c + 1) * size, p:p + 1], gmix[srows, a:a + 128])
            gq[srows, a:a + 128] = of_q.astype(BF16)
            gkv[krows, a:a + 128], gkv[krows, b:b + 128] = of_k.astype(BF16), of_v.astype(BF16)
    yield 1.0
    vec[9:10, :] = column_sum(gq[...])
    vec[10:11, :] = column_sum(gkv[:, D:])
    gn[...] = dot(gq[...], tiles[0], NT)
    yield 1.5
    norm_backward(f.h.at[0], rows[1:2, :], gn, g, vec, 1, 4)
    f.stage = 1
    yield 1.0
    gb = f.gb.at[0]
    gb[...] = g[...].astype(BF16)
    vec[8:9, :] = column_sum(gb[...])
    gmix[...] = dot(gb[...], tiles[7], NT).astype(BF16)
    need(("packed", 0), ("logsum", 0))
    packed, logsum = f.packed.at[0], f.logsum.at[0]
    for p in range(D // 128):
        if p % 3 == 0:
            yield 3.0
        seen = f.allowed[...] != 0
        seen = jnp.concatenate([seen, seen], axis=0)
        a = p * 128
        q, k, v = (slice(t * D + a, t * D + a + 128) for t in range(3))
        of_q, of_k, of_v = attend_back(
            packed[:, q], packed[:, k], packed[:, v], seen, logsum[:, p:p + 1], gmix[:, a:a + 128])
        gpacked[:, q], gpacked[:, k], gpacked[:, v] = of_q.astype(BF16), of_k.astype(BF16), of_v.astype(BF16)
    yield 2.0
    vec[6:7, :] = column_sum(gpacked[:, :D])
    vec[7:8, :] = column_sum(gpacked[:, 2 * D:])
    gn[...] = dot(gpacked[:, :D], tiles[4], NT) + dot(gpacked[:, D:2 * D], tiles[5], NT) + dot(gpacked[:, 2 * D:], tiles[6], NT)
    yield 1.5
    norm_backward(f.tokens, rows[0:1, :], gn, g, vec, 0, 3)
    f.stage = 2
    for i in range(near // 2):
        yield 1.5
        krows = slice(2 * i * length, 2 * (i + 1) * length)
        value = dot(gkv[krows, :D], tiles[1], NT) + dot(gkv[krows, D:], tiles[2], NT)
        near_out(i, value.reshape(2, length, D))
    f.stage = 3


def scatter_routes(parts, width):
    if parts == 1:
        return [(ROUTES[0][0][::-1], 0, 1, 0, width)]
    third = width // 3
    cut = ((0, 1, 0), (1, 1, 0), (0, 2, third), (0, 2, 2 * third))
    return [(order[::-1], *where, third) for (order, _), where in zip(ROUTES, cut)]


def scatter_kernel(dp_size, fsdp_size, chunks, count, plan, spans, *refs):
    factors = dict(zip(FACTORS, refs[:11]))
    (first, near, near_tokens, rows, tokens, segments, g_in, vec_in, vec_up) = refs[11:20]
    outs, grad_tokens, grad_near = refs[20:20 + count], refs[20 + count], refs[21 + count]
    refs = refs[22 + count:]
    f = types.SimpleNamespace(**dict(zip(FACTORS, refs[:11])))
    (f.gq, f.gkv, f.tiles, f.gmix, f.gn, f.vec, f.allowed, small, near_stage), scratch = refs[11:20], refs[20:-5]
    brought, loads, near_sem, send, recv = refs[-5:]
    f.near, f.near_tokens, f.rows, f.tokens, f.g, f.stage = near, near_tokens, rows, tokens, grad_tokens, 0
    D = tokens.shape[1]
    place = Place(dp_size, fsdp_size)
    sems = Sems(send, recv)
    c = place.at["c"]
    sibling = place.device("c", 1 - c)
    arriving = {}

    def bring(number):
        name, index, slot = (ORDER + LATER)[number]
        copy = pltpu.make_async_copy(factors[name].at[index], getattr(f, name).at[slot], brought.at[number])
        copy.start()
        arriving[name, index] = [copy]

    def load(j):
        copy = pltpu.make_async_copy(first.at[:, (j + 4) % 8 * D:((j + 4) % 8 + 1) * D], f.tiles.at[j], loads.at[j])
        copy.start()
        return copy
    for number in range(4):
        bring(number)
    arriving["tiles", 0] = [load(j) for j in range(8)]
    for number in range(4, len(ORDER)):
        bring(number)

    def need(*wanted):
        for key in wanted:
            for copy in arriving.pop(key, ()):
                copy.wait()
    near_copies = []

    def near_out(i, value):
        if near_copies:
            near_copies.pop().wait()
        near_stage[...] = value
        near_copies.append(pltpu.make_async_copy(near_stage, grad_near.at[2 * i:2 * i + 2], near_sem))
        near_copies[-1].start()
    chain = chain_pieces(f, need, near_out, spans)

    def require(stage):
        while f.stage < stage:
            next(chain)
    makers = chunk_makers(f, need, lambda number: bring(len(ORDER) + number), require)
    everything = pl.ds(0, place.size["y"])
    lead = tuple(place.size[name] for name in NAMES if name != "c")

    def pack():
        require(2)
        part, wide = outs[-1].shape[0], vec_up.shape[1]
        for index in itertools.product(*(range(place.size[name]) for name in NAMES)):
            i = ((index[0] * 2 + index[1]) * place.size["z"] + index[2]) * 2 + index[3]
            devices = dp_size * fsdp_size
            one, many = D // devices, wide // devices
            values = jnp.pad(f.vec[0:21, i * one:(i + 1) * one], ((0, 0), (0, 128 - one)))
            ups = jnp.pad(vec_up[0:2, i * many:(i + 1) * many], ((0, 0), (0, 128 - many)))
            blank = jnp.zeros((part - 23, 128), F32)
            small[(*index, 0)] = jnp.concatenate([values, ups, blank], axis=0).astype(BF16)

    def chunk_flow(make, grad, landing, buffers, routed, targets):
        if make is not None:
            make()
        crossing = []
        for _, j, nj, col, width in routed:
            slot, part = sems.take(), (pl.ds(j, nj), slice(None), pl.ds(col, width))
            copy = sems.copy(slot, grad.at[(everything, 1 - c, slice(None), slice(None), *part)],
                             landing.at[(slice(None), slice(None), slice(None), *part)], sibling)
            copy.start()
            crossing.append(copy)
        yield
        for copy in crossing:
            copy.wait()
        add_blocks(lead + landing.shape[3:4], landing, landing, grad.at[:, c])
        flows = []
        for (order, j, nj, col, width), own in zip(routed, buffers):
            part = (pl.ds(j, nj), slice(None), pl.ds(col, width))
            flows.append(scatter_flow(
                place, sems, landing.at[(slice(None), slice(None), slice(None), *part)], own, order,
                [target.at[:, pl.ds(col, width)] for target in targets[j:j + nj]], (nj,)))
        while flows:
            flows = [flow for flow in flows if next(flow, 0) is None]
            if flows:
                yield

    groups = []
    for number, (group, places) in enumerate(zip(chunks, plan)):
        members = []
        for (which, row, height, col, width), (grad, landing, buffers) in zip(group, places):
            if grad is None:
                make, array, targets = pack, small, [outs[which]]
            else:
                make, array = makers[number], scratch[grad]
                fill = [array]
                if makers[(number + 1) % len(makers)] is None:
                    fill = [scratch[plan[number + 1][0][0]], array]
                make = make and functools.partial(make, fill)
                rows_, cols_ = array.shape[5:]
                if width == cols_:
                    targets = [outs[which].at[row + j * rows_:row + (j + 1) * rows_, :] for j in range(2)]
                else:
                    targets = [outs[which].at[:, col + j * cols_:col + (j + 1) * cols_] for j in range(2)]
            members.append(chunk_flow(
                make, array, scratch[landing], [[scratch[b] for b in own] for own in buffers],
                scatter_routes(array.shape[4], array.shape[6]), targets))
        groups.append(members)

    fill_allowed(f.allowed, segments)
    grad_tokens[...] = g_in[...]
    f.vec[...] = vec_in[...]
    greet(place)

    def chain_some(tick):
        left = CHAIN_SHARE
        while f.stage < 3 and left > 0 and (f.stage != 1 or tick >= 5):
            left -= next(chain, 9.0)
    run_schedule(groups, SCATTER_STEPS, chain_some)
    require(3)
    sems.drain()
    near_copies.pop().wait()


def scatter_all(mesh_shape, factors, first, near, near_tokens, rows, tokens, segment_ids, g, vec, vec_up, spans, owned, chunks,
                collective_id):
    dp_size, fsdp_size = mesh_shape
    size = {"y": dp_size // 2, "c": 2, "z": fsdp_size // 2, "x": 2}
    lead = tuple(size[name] for name in NAMES if name != "c")
    whole = tuple(size[name] for name in NAMES)
    T, D = tokens.shape
    count_near, length, _ = near.shape
    part = D // (dp_size * fsdp_size)
    shapes, plan, pools, count = [], [], {}, 0

    def new(shape, role, most):
        pool = pools.setdefault((shape, role), [])
        if len(pool) < most:
            shapes.append(pltpu.VMEM(shape, BF16))
            pool.append(len(shapes) - 1)
        else:
            pool.append(pool.pop(0))
        return pool[-1]

    for group in chunks:
        places = []
        for which, *_ in group:
            small = which == len(owned) - 1
            block = (1, 32, 128) if small else (2, part, D)
            grad = None if small else new(whole + block, 0, 3)
            landing = new(lead + block, 1, LANDINGS)
            buffers = []
            for number, (order, _, nj, _, width) in enumerate(scatter_routes(block[0], block[2])):
                buffers.append([
                    new(s, (2, number, i), WINDOW)
                    for i, s in enumerate(scatter_buffers(size, order, (nj, block[1], width)))])
                count += copies_of(order, size)
            places.append((grad, landing, buffers))
        plan.append(places)
    vmem, hbm = pl.BlockSpec(memory_space=pltpu.VMEM), pl.BlockSpec(memory_space=pl.ANY)
    slots = {"active": 1, "gh": 1, "gpacked": 1, "packed": 1, "h": 1}
    return pl.pallas_call(
        functools.partial(scatter_kernel, dp_size, fsdp_size, chunks, len(owned), plan, spans),
        out_shape=[jax.ShapeDtypeStruct(shape, F32) for shape in (*owned, (T, D), near.shape)],
        in_specs=[hbm] * 12 + [vmem] * 8,
        out_specs=[vmem] * (len(owned) + 1) + [hbm],
        scratch_shapes=[
            pltpu.VMEM((slots.get(name, factors[name].shape[0]),) + factors[name].shape[1:], factors[name].dtype)
            for name in FACTORS
        ] + [
            pltpu.VMEM((T, D), BF16), pltpu.VMEM((count_near * length, 2 * D), BF16), pltpu.VMEM((8, D, D), BF16),
            pltpu.VMEM((T, D), BF16), pltpu.VMEM((T, D), F32), pltpu.VMEM((24, D), F32), pltpu.VMEM((T, T), jnp.int32),
            pltpu.VMEM(whole + (1, 32, 128), BF16), pltpu.VMEM((2, length, D), F32),
        ] + shapes + [
            pltpu.SemaphoreType.DMA((len(ORDER) + len(LATER),)),
            pltpu.SemaphoreType.DMA((8,)),
            pltpu.SemaphoreType.DMA,
            pltpu.SemaphoreType.DMA((count,)),
            pltpu.SemaphoreType.DMA((count,)),
        ],
        compiler_params=pltpu.CompilerParams(
            collective_id=collective_id, has_side_effects=True, vmem_limit_bytes=VMEM_MOST),
        name="scatter_gradients",
    )(*[factors[name] for name in FACTORS], first, near, near_tokens, rows, tokens, segment_ids,
      g, vec, vec_up)


PLACES = ((0, 0), (0, 3), (0, 4), (0, 5), (0, 7), (1, 0), (2, 0), (3, 0), (3, 3), (4, 0), (5, 0))


def chunk_table(D, part, long):
    table = [((0, 0, part, i * 2 * D, 2 * D),) for i in range(4)]
    for first in (1, 3):
        if first == 3:
            table += [((3, 0, part, i * 2 * D, 2 * D),) for i in range(2)]
        table += [((first + first // 3, 0, part, i * 2 * D, 2 * D),) for i in range(2)]
        table += [((first + first // 3 + 1, i * long // 2, long // 2, 0, D),) for i in range(2)]
    table[0] += ((6, 0, 32, 0, 128),)
    return table


def local(mesh_shape, *arrays):
    (tokens, segment_ids, neighbours, neighbour_ids, neighbour_tokens, gains_one, biases_one, w_qkv_one, w_out_one,
     w_cross_q, w_cross_kv, w_cross_out, w_up_one, bias_up_one, w_down_one, gains_two, biases_two, w_qkv_two,
     w_out_two, w_up_two, bias_up_two, w_down_two, cotangent) = arrays
    row_count, D = tokens.shape
    FF = w_up_one.shape[1]
    devices = mesh_shape[0] * mesh_shape[1]
    part = D // devices
    quarter = FF // D
    vectors = [gains_one, biases_one, gains_two, biases_two]
    shards = [w_qkv_one, w_out_one, w_cross_q, w_cross_kv, w_cross_out, w_up_one, w_down_one, w_qkv_two, w_out_two,
              w_up_two, w_down_two]
    kernels = part % 8 == 0
    table = chunk_table(D, part, w_down_one.shape[0])
    store_count = neighbours.shape[0]
    spans = neighbour_ids.shape[1]
    near_index = neighbour_ids.reshape(-1) % store_count
    if kernels:
        ups = [bias_up_one.reshape(1, -1), bias_up_two.reshape(1, -1)]
        near, near_tokens = arrange(near_index, neighbours, neighbour_tokens)
        wholes, (out, h, rows), saved = gather_and_run(
            mesh_shape, shards, tuple((w, c * D) for w, c in PLACES), vectors + ups, table, tokens, segment_ids,
            near, near_tokens, spans, 1)
        wholes = [w.reshape(-1, w.shape[-1]) for w in wholes]
        (gradient, vec, vec_up), made = run_backward(cotangent, segment_ids, rows, h, saved, wholes[1:])
        owned = [(w.shape[0] // devices, w.shape[1]) for w in wholes] + [(32, 128)]
        *owned, gradient, grad_neighbours = scatter_all(
            mesh_shape, {**saved, **made, "h": h}, wholes[0], near, near_tokens, rows, tokens, segment_ids, gradient, vec, vec_up,
            spans, owned, table[::-1], 2)
    else:
        small = jnp.concatenate(vectors + [bias_up_one.reshape(-1, part), bias_up_two.reshape(-1, part)])
        small = jnp.pad(small, ((0, -small.shape[0] % 32), (0, -part % 128)))
        sides = [[] for _ in range(6)]
        for shard, (which, _) in zip(shards, PLACES):
            sides[which].append(shard)
        shards = [jnp.concatenate(side, axis=1) for side in sides] + [small]
        *wholes, smalls = [lax.all_gather(s, ("dp", "fsdp"), axis=0, tiled=True) for s in shards]
        smalls = smalls.reshape(devices, -1, smalls.shape[-1])[:, :, :part]
        rows = smalls[:, :21].transpose(1, 0, 2).reshape(21, D)
        bias_up = [smalls[:, 21 + i * quarter:21 + (i + 1) * quarter].reshape(FF) for i in range(2)]
        rows = jnp.pad(rows.astype(F32), ((0, 3), (0, 0)))
        bias_up = jnp.pad(jnp.stack(bias_up).astype(F32), ((0, 6), (0, 0)))
        out, gradient, grad_neighbours, *grads, vectors, vectors_up = run_blocks(
            tokens, cotangent, segment_ids, neighbours, near_index, neighbour_tokens, spans, rows, bias_up, wholes)
        vectors = vectors[:21].reshape(21, devices, part).transpose(1, 0, 2)
        ups = vectors_up[:2].reshape(2, devices, quarter * part).transpose(1, 0, 2)
        vectors = [jnp.pad(v, ((0, 0), (0, 0), (0, 128 - v.shape[2]))) for v in (vectors, ups)]
        vectors = jnp.pad(jnp.concatenate(vectors, axis=1), ((0, 0), (0, 9), (0, 0)))
        grads.append(vectors.reshape(-1, 128).astype(BF16))
        owned = [lax.psum_scatter(g.astype(F32), ("dp", "fsdp"), scatter_dimension=0, tiled=True) for g in grads]
        grad_neighbours = jnp.take(grad_neighbours, near_index, axis=0)
    *split, grad_neighbours = split_gradients(owned, grad_neighbours, near_index, D, quarter, part)
    split[8], split[15] = split[8].reshape(-1), split[15].reshape(-1)
    return (out, gradient, grad_neighbours, *split)


def solution(mesh):
    in_specs = (
        P(("dp", "fsdp"), None),
        P(("dp", "fsdp"), None),
        P(("dp", "fsdp"), None, None),
        P(("dp", "fsdp"), None, None),
        P(("dp", "fsdp"), None),
        P(None, ("dp", "fsdp")),
        P(None, ("dp", "fsdp")),
        P(("dp", "fsdp"), None),
        P(("dp", "fsdp"), None),
        P(("dp", "fsdp"), None),
        P(("dp", "fsdp"), None),
        P(("dp", "fsdp"), None),
        P(("dp", "fsdp"), None),
        P(("dp", "fsdp")),
        P(("dp", "fsdp"), None),
        P(None, ("dp", "fsdp")),
        P(None, ("dp", "fsdp")),
        P(("dp", "fsdp"), None),
        P(("dp", "fsdp"), None),
        P(("dp", "fsdp"), None),
        P(("dp", "fsdp")),
        P(("dp", "fsdp"), None),
        P(("dp", "fsdp"), None),
    )
    out_specs = (
        P(("dp", "fsdp"), None),
        P(("dp", "fsdp"), None),
        P(("dp", "fsdp"), None, None),
        P(None, ("dp", "fsdp")),
        P(None, ("dp", "fsdp")),
        P(("dp", "fsdp"), None),
        P(("dp", "fsdp"), None),
        P(("dp", "fsdp"), None),
        P(("dp", "fsdp"), None),
        P(("dp", "fsdp"), None),
        P(("dp", "fsdp"), None),
        P(("dp", "fsdp")),
        P(("dp", "fsdp"), None),
        P(None, ("dp", "fsdp")),
        P(None, ("dp", "fsdp")),
        P(("dp", "fsdp"), None),
        P(("dp", "fsdp"), None),
        P(("dp", "fsdp"), None),
        P(("dp", "fsdp")),
        P(("dp", "fsdp"), None),
    )
    return jax.shard_map(
        functools.partial(local, (mesh.shape["dp"], mesh.shape["fsdp"])), mesh=mesh, in_specs=in_specs, out_specs=out_specs, check_vma=False)
```

time: 2270 us -> 356 us (0.16)
  waiting for transfers between devices: 1540 us -> 0 us
  Pallas kernels: 0 us -> 348 us
  blocking collectives: 304 us -> 0 us
  local copies, waits for them, and re-layouts: 195 us -> 3.5 us
  matrix products: 165 us -> 0 us
  other arithmetic: 40 us -> 0.52 us
    reduce_scatter x11 -> x0, waiting for transfers between devices: 1270 us -> none  [the longest x1 140 us: local(): lax.psum_scatter(flat_rows(grad_w_up_b), ('dp', 'fsdp'), scatter_dimensio...]
    pallas_call x0 -> x5, Pallas kernels: none -> 348 us  [the longest x1 158 us: scatter_all(): pl.pallas_call(functools.partial(scatter_kernel, dp_size, fsdp_size, chun...]
    all_gather x4 -> x0, blocking collectives: 267 us -> none  [the longest x1 71.1 us: local(): lax.all_gather(biases_one, ('dp', 'fsdp'), axis=1, tiled=True)]
    all_gather x11 -> x0, waiting for transfers between devices: 264 us -> none  [the longest x1 60.9 us: local(): lax.all_gather(w_down_two, ('dp', 'fsdp'), axis=0, tiled=True)]
    dot_general x51 -> x0, matrix products: 165 us -> none  [the longest x33 137 us: product(): return jnp.dot(left, right, preferred_element_type=jnp.float32)]
    reshape x39 -> x1, local copies, waits for them, and re-layouts: 120 us -> 0.08 us  [local(): near_index = neighbour_ids.reshape(-1) % store_count]
    unnamed x1 -> x0, blocking collectives: 37.2 us -> none
    unnamed x314 -> x5, local copies, waits for them, and re-layouts: 30.7 us -> 3.42 us
  transfers between devices with their start and end apart: 23 -> 0, of which waited for: 16 -> 0; matrix products, arithmetic and copies ran while one was open for 12% -> 0% of each run, Pallas kernels for 0% -> 0%
where the time goes in v1:
time: 356 us; the launch traced here: 353 us
  Pallas kernels  348 us (98%)
    pallas_call x1, Pallas kernels, scatter_all(): pl.pallas_call(functools.partial(scatter_kernel, dp_size, fsdp_size, chun...  158 us
    pallas_call x1, Pallas kernels, gather_and_run(): pl.pallas_call(functools.partial(forward_kernel, dp_size, fsdp_size, chun...  157 us
    pallas_call x1, Pallas kernels, run_backward(): pl.pallas_call(backward_kernel, out_shape=[shape((T, D), F32), shape((24,...  24 us

profile of v1, /device:TPU:0, one launch (start us, length us, event | category | flops | bytes accessed | tf_op | source)
XLA Modules:
  0.0 353.0 jit_solution(4732057413232632978)
XLA Ops:
  0.7 0.8 copy.44
  1.4 0.1 reshape.75
  1.5 0.5 and_select_fusion.ids.refs_8_
  2.0 3.4 arrange_neighbours.1
  5.4 157.3 %gather_and_forward.1 = (bf16[2,2,4,2,24,6144]{5,4,3,2,1,0:T(8,128)(2,1)}, bf16[2,2,4,2,24,3072]{5,4,3,2,1,0:T(8,128)(2,1)}, bf16[2,2,4,2,96,768]{5,4,3,2,1,0:T(...) custom-call(bf16[24,2304]{1,0:T(8,128)(2,1)} %refs_0_.2, ...), custom_call_target="tpu_custom_call" | custom-call | tf_op jit(solution)/shard_map/gather_and_forward/pallas_call | solution.py:1025
  162.7 24.0 %backward.1 = (f32[256,768]{1,0:T(8,128)}, f32[24,768]{1,0:T(8,128)}, f32[8,3072]{1,0:T(8,128)}, bf16[5,256,768]{2,1,0:T(8,128)(2,1)}, bf16[2,256,3072]{2,1,0:T(8,128)(2,1)}, /*index=5*/bf16[2,256,2304]{2,1,0:T(8,128)(2,1)}) custom-call(bf16[256,768]{1,0:T(8,128)(2,1)} %refs_0_.3, s32[1,256]{1,0:T(1,128)} %refs_16_.1, ...), custom_call_target="tpu_custom_call" | custom-call | tf_op jit(solution)/shard_map/backward/pallas_call | solution.py:1165
  186.7 157.7 %scatter_gradients.1 = (f32[24,6144]{1,0:T(8,128)}, f32[24,3072]{1,0:T(8,128)}, f32[96,768]{1,0:T(8,128)}, f32[24,3072]{1,0:T(8,128)}, f32[24,3072]{1,0:T(8,128)...) custom-call(bf16[5,256,768]{2,1,0:T(8,128)(2,1)} %get-tuple-element.75.refs_0_, ...), custom_call_target="tpu_custom_call" | custom-call | tf_op jit(solution)/shard_map/scatter_gradients/pallas_call | solution.py:1511
  344.4 0.0 copy-start
  344.5 5.7 %split_gradients.1 = (f32[3,24]{1,0:T(4,128)}, f32[10,24]{1,0:T(8,128)}, f32[24,2304]{1,0:T(8,128)}, f32[24,768]{1,0:T(8,128)}, f32[24,768]{1,0:T(8,128)}, /*ind...) custom-call(f32[24,6144]{1,0:T(8,128)} %get-tuple-element.98.refs_0_, ...), custom_call_target="tpu_custom_call" | custom-call | tf_op jit(solution)/shard_map/split_gradients/pallas_call | solution.py:304
  350.1 1.8 copy.47
  351.9 0.0 copy-done
  351.9 0.9 copy.48
Async XLA Ops:
  344.4 7.5 %copy-start = (f32[256,768]{1,0:T(8,128)S(1)}, f32[256,768]{1,0:T(8,128)}, u32[]{:S(2)}) copy-start(f32[256,768]{1,0:T(8,128)} %get-tuple-element.145) | copy-start | bytes 2359300

commit v2 on v1

--- a/solution.py
+++ b/solution.py
@@ -16,7 +16,7 @@
 NAMES = ("y", "c", "z", "x")
 GATHER_STEPS = (0, 1, 2, 3, 4, 6, 8)
 VMEM_MOST = 63 * 2 ** 20
-COMPUTE_SHARE, CHAIN_SHARE = 3.5, 3.0
+COMPUTE_SHARE, CHAIN_SHARE = 3.5, 3.5
 SCATTER_STEPS = (0, 2, 4, 5, 6, 7, 8)
 LANDINGS, WINDOW = 6, 8
 
@@ -1064,119 +1064,48 @@
     norm_backward(h_in, gain, gn, g, vec, rows[0], rows[1])
 
 
-def self_chain(e, i, h_in, w, gain, norm, rows):
-    D = h_in.shape[1]
-    packed, logsum, gb, gpacked = e.packed.at[i], e.logsum.at[i], e.gb.at[norm], e.gpacked.at[i]
-    g, gmix, gn, vec = e.g, e.gmix, e.gn, e.vec
-    gb[...] = g[...].astype(BF16)
-    vec[rows[4]:rows[4] + 1, :] = column_sum(gb[...])
-    e.save("gb", norm)
-    gmix[...] = dot(gb[...], w[:, 3 * D:4 * D], NT).astype(BF16)
-    seen = e.allowed[...] != 0
-    seen = jnp.concatenate([seen, seen], axis=0)
-    for p in range(D // 128):
-        a = p * 128
-        q, k, v = (slice(t * D + a, t * D + a + 128) for t in range(3))
-        of_q, of_k, of_v = attend_back(
-            packed[:, q], packed[:, k], packed[:, v], seen, logsum[:, p:p + 1], gmix[:, a:a + 128])
-        gpacked[:, q], gpacked[:, k], gpacked[:, v] = of_q.astype(BF16), of_k.astype(BF16), of_v.astype(BF16)
-    e.save("gpacked", i)
-    vec[rows[2]:rows[2] + 1, :] = column_sum(gpacked[:, :D])
-    vec[rows[3]:rows[3] + 1, :] = column_sum(gpacked[:, 2 * D:])
-    gn[...] = jnp.zeros_like(gn)
-
-    def back(j):
-        cols = span_of(j, D)
-        gn[...] += dot(gpacked[:, cols], w[:, cols], NT)
-    pl.loop(0, 3)(back)
-    norm_backward(h_in, gain, gn, g, vec, rows[0], rows[1])
-
-
-KEPT = ("packed", "logsum", "slope")
-MADE = ("gb", "gh", "gpacked")
-
-
 def backward_kernel(*refs):
-    (cotangent, segments, rows, h_in, up_a, down_a, second, up_b, down_b) = refs[:9]
-    stored = dict(zip(KEPT, refs[9:12]))
-    g, vec, vec_up = refs[12:15]
-    given, held, made = dict(zip(MADE, refs[15:18])), dict(zip(KEPT, refs[18:21])), dict(zip(MADE, refs[21:24]))
-    (h, allowed, gmix, gn, wide, tall, loads, brought, saves) = refs[24:]
-
-    def load(number):
-        src, dst = (
-            (down_b, tall.at[1]), (up_b, wide.at[1]), (second, wide.at[0]), (down_a, tall.at[0]), (up_a, wide.at[2]))[number]
-        return pltpu.make_async_copy(src, dst, loads.at[number])
-
-    wanted = ((2, 1), (3, 3), (0, 1), (1, 1), (3, 2), (2, 0), (3, 1))
-
-    def bring(number):
-        which, index = wanted[number]
-        src, dst = (h_in, h) if which == 3 else (stored[KEPT[which]], held[KEPT[which]])
-        return pltpu.make_async_copy(src.at[index], dst.at[index], brought.at[number])
-
+    cotangent, rows, h_in, slope_in, up, down, g, vec, vec_up, gb_out, gh_out, slope, gb, gh, h, gn, wide, tall, brought, saves = refs
+    copies = [
+        pltpu.make_async_copy(src, dst, brought.at[i])
+        for i, (src, dst) in enumerate(((down, tall), (slope_in.at[1], slope.at[0]), (up, wide), (h_in.at[3], h)))]
+    for copy in copies:
+        copy.start()
     saved = []
 
     def save(name, index):
-        copy = pltpu.make_async_copy(made[name].at[index], given[name].at[index], saves.at[len(saved)])
+        src, dst = (gb.at[4], gb_out.at[4]) if name == "gb" else (gh.at[0], gh_out.at[1])
+        copy = pltpu.make_async_copy(src, dst, saves.at[len(saved)])
         copy.start()
         saved.append(copy)
-
-    load(0).start()
-    bring(0).start()
-    load(1).start()
-    bring(1).start()
-    load(2).start()
-    for number in range(2, len(wanted)):
-        bring(number).start()
-    load(3).start()
-    load(4).start()
-    fill_allowed(allowed, segments)
-    e = types.SimpleNamespace(**held, **made, allowed=allowed, g=g, gmix=gmix, gn=gn, vec=vec, vec_up=vec_up, save=save)
-
-    def row(i):
-        return rows[i:i + 1, :]
-
-    def ready(*numbers):
-        for number in numbers:
-            bring(number).wait()
+    e = types.SimpleNamespace(slope=slope, gb=gb, gh=gh, g=g, gn=gn, vec=vec, vec_up=vec_up.at[1:2], save=save)
     g[...] = cotangent[...].astype(F32)
-    load(0).wait()
-    load(1).wait()
-    ready(0, 1)
-    ffn_chain(e, 1, h.at[3], wide.at[1], tall.at[1], row(14), 4, (14, 16, 20))
-    load(2).wait()
-    ready(2, 3, 4)
-    self_chain(e, 1, h.at[2], wide.at[0], row(13), 3, (13, 15, 17, 18, 19))
-    load(3).wait()
-    load(4).wait()
-    ready(5, 6)
-    ffn_chain(e, 0, h.at[1], wide.at[2], tall.at[0], row(2), 2, (2, 5, 12))
+    for copy in copies:
+        copy.wait()
+    ffn_chain(e, 0, h, wide, tall, rows[14:15, :], 4, (14, 16, 20))
     for copy in saved:
         copy.wait()
 
 
-def run_backward(cotangent, segment_ids, rows, h, saved, weights):
+def run_backward(cotangent, rows, h, slope, w_up, w_down):
     T, D = cotangent.shape
     FF = 4 * D
     vmem, hbm = pl.BlockSpec(memory_space=pltpu.VMEM), pl.BlockSpec(memory_space=pl.ANY)
     shape = jax.ShapeDtypeStruct
-    made = ((5, T, D), (2, T, FF), (2, T, 3 * D))
     results = pl.pallas_call(
         backward_kernel,
-        out_shape=[shape((T, D), F32), shape((24, D), F32), shape((8, FF), F32)] + [shape(s, BF16) for s in made],
-        in_specs=[vmem] * 3 + [hbm] * 9,
-        out_specs=[vmem] * 3 + [hbm] * 3,
-        scratch_shapes=[pltpu.VMEM(saved[name].shape, saved[name].dtype) for name in KEPT]
-        + [pltpu.VMEM(s, BF16) for s in made] + [
-            pltpu.VMEM((4, T, D), F32), pltpu.VMEM((T, T), jnp.int32), pltpu.VMEM((T, D), BF16),
-            pltpu.VMEM((T, D), F32), pltpu.VMEM((3, D, FF), BF16), pltpu.VMEM((2, FF, D), BF16),
-            pltpu.SemaphoreType.DMA((5,)), pltpu.SemaphoreType.DMA((7,)), pltpu.SemaphoreType.DMA((6,)),
+        out_shape=[shape((T, D), F32), shape((24, D), F32), shape((8, FF), F32), shape((5, T, D), BF16), shape((2, T, FF), BF16)],
+        in_specs=[vmem] * 2 + [hbm] * 4,
+        out_specs=[vmem] * 3 + [hbm] * 2,
+        scratch_shapes=[
+            pltpu.VMEM((1, T, FF), BF16), pltpu.VMEM((5, T, D), BF16), pltpu.VMEM((1, T, FF), BF16), pltpu.VMEM((T, D), F32),
+            pltpu.VMEM((T, D), F32), pltpu.VMEM((D, FF), BF16), pltpu.VMEM((FF, D), BF16),
+            pltpu.SemaphoreType.DMA((4,)), pltpu.SemaphoreType.DMA((2,)),
         ],
         compiler_params=pltpu.CompilerParams(vmem_limit_bytes=VMEM_MOST, has_side_effects=True),
         name="backward",
-    )(cotangent, segment_ids, rows, h, *weights, *[saved[name] for name in KEPT])
-    return results[:3], dict(zip(MADE, results[3:]))
+    )(cotangent, rows, h, slope, w_up, w_down)
+    return results[:3], {"gb": results[3], "gh": results[4]}
 
 
 def gradient_columns(dst, j, left, right, right_col):
@@ -1205,11 +1134,12 @@
     pl.loop(0, left.shape[1] // each)(block)
 
 
-FACTORS = ("n", "active", "mixed", "gb", "gh", "gpacked", "packed", "logsum", "kv", "queries", "h")
-ORDER = (("active", 1, 0), ("gb", 4, 4), ("n", 4, 4), ("gh", 1, 0), ("kv", 0, 0), ("queries", 0, 0), ("logsum", 2, 2), ("h", 0, 0),
-         ("n", 3, 3), ("gpacked", 1, 0), ("mixed", 1, 1), ("gb", 3, 3), ("packed", 0, 0), ("logsum", 0, 0), ("gb", 2, 2),
-         ("n", 2, 2), ("n", 1, 1), ("mixed", 2, 2), ("n", 0, 0), ("mixed", 0, 0))
-LATER = (("active", 0, 0), ("gh", 0, 0))
+FACTORS = ("n", "active", "mixed", "gb", "gh", "packed", "logsum", "kv", "queries", "h", "slope")
+ORDER = (("active", 1, 0), ("gb", 4, 4), ("packed", 1, 0), ("logsum", 1, 0), ("h", 2, 0), ("n", 4, 0), ("gh", 1, 0), ("n", 3, 1),
+         ("mixed", 1, 0), ("slope", 0, 0), ("n", 2, 2), ("kv", 0, 0), ("queries", 0, 0), ("mixed", 2, 1))
+LATER = (("active", 0, 0), ("n", 1, 0), ("packed", 0, 0), ("logsum", 2, 0), ("h", 1, 0), ("h", 0, 0), ("logsum", 0, 0), ("n", 0, 1),
+         ("mixed", 0, 0))
+SLOTS = {("n", 4): 0, ("n", 3): 1, ("n", 2): 2, ("n", 1): 0, ("n", 0): 1, ("mixed", 1): 0, ("mixed", 2): 1, ("mixed", 0): 0}
 
 
 def chunk_makers(f, need, later, require):
@@ -1218,6 +1148,7 @@
 
     def rows_of(i, norm):
         def make(dsts):
+            require(2 - 2 * i)
             need(("active", i), ("gb", norm))
             gradient_rows(dsts, f.active.at[0], f.gb.at[norm])
             if i:
@@ -1226,10 +1157,11 @@
 
     def columns(dst, j, name, index, right, right_col):
         left = getattr(f, name)
-        gradient_columns(dst, j, lambda rows: left[index, :, rows], right, right_col)
+        gradient_columns(dst, j, lambda rows: left[SLOTS[name, index], :, rows], right, right_col)
 
     def up(i, norm, half):
         def make(dsts):
+            require(2 - 2 * i)
             need(("n", norm), ("gh", i))
             for j in range(2):
                 columns(dsts[0], j, "n", norm, f.gh.at[0], (2 * half + j) * D)
@@ -1239,53 +1171,113 @@
 
     def query_key(i, norm):
         def make(dsts):
-            require(2 - 2 * i)
-            need(("n", norm), ("gpacked", i))
+            require(4 - 3 * i)
+            need(("n", norm),)
             for j in range(2):
-                columns(dsts[0], j, "n", norm, f.gpacked.at[0], j * D)
+                columns(dsts[0], j, "n", norm, f.gpacked, j * D)
+            if i:
+                later(7)
         return make
 
     def value_out(i, norm):
         def make(dsts):
-            require(2 - 2 * i)
-            need(("n", norm), ("gpacked", i), ("mixed", i), ("gb", norm))
-            columns(dsts[0], 0, "n", norm, f.gpacked.at[0], 2 * D)
+            require(4 - 3 * i)
+            need(("n", norm), ("mixed", i))
+            columns(dsts[0], 0, "n", norm, f.gpacked, 2 * D)
             columns(dsts[0], 1, "mixed", i, f.gb.at[norm], 0)
+            if i:
+                later(8)
         return make
 
     def near_rows(rows):
         return near[:, :, rows].reshape(-1, rows.size)
 
     def cross_one(dsts):
-        require(1)
-        need(("n", 1))
+        require(3)
+        need(("n", 1),)
         columns(dsts[0], 0, "n", 1, f.gq, 0)
         gradient_columns(dsts[0], 1, near_rows, f.gkv, 0)
 
     def cross_two(dsts):
-        require(1)
-        need(("mixed", 2))
+        require(3)
+        need(("mixed", 2),)
         gradient_columns(dsts[0], 0, near_rows, f.gkv, D)
         columns(dsts[0], 1, "mixed", 2, f.gb.at[1], 0)
     return (rows_of(1, 4), None, up(1, 4, 1), up(1, 4, 0), value_out(1, 3), query_key(1, 3), rows_of(0, 2), None,
             up(0, 2, 1), up(0, 2, 0), cross_two, cross_one, value_out(0, 0), query_key(0, 0))
 
 
-def chain_pieces(f, need, near_out, spans):
-    g, gn, gmix, vec, rows, gq, gkv, gpacked = f.g, f.gn, f.gmix, f.vec, f.rows, f.gq, f.gkv, f.gpacked.at[0]
+def self_back_pieces(f, need, norm, gain, h, lines):
+    g, gn, gmix, vec, gpacked, tiles = f.g, f.gn, f.gmix, f.vec, f.gpacked, f.tiles
     D = g.shape[1]
-    tiles = f.tiles
+    of_gain, of_shift, of_q, of_v, of_out = (slice(line, line + 1) for line in lines)
+    gb = f.gb.at[norm]
+    gb[...] = g[...].astype(BF16)
+    vec[of_out, :] = column_sum(gb[...])
+    gmix[...] = dot(gb[...], tiles[3], NT).astype(BF16)
+    packed, logsum = f.packed.at[0], f.logsum.at[0]
+    for p in range(D // 128):
+        if p % 3 == 0:
+            yield 3.0
+        seen = f.allowed[...] != 0
+        seen = jnp.concatenate([seen, seen], axis=0)
+        a = p * 128
+        q, k, v = (slice(t * D + a, t * D + a + 128) for t in range(3))
+        grad_q, grad_k, grad_v = attend_back(
+            packed[:, q], packed[:, k], packed[:, v], seen, logsum[:, p:p + 1], gmix[:, a:a + 128])
+        gpacked[:, q], gpacked[:, k], gpacked[:, v] = grad_q.astype(BF16), grad_k.astype(BF16), grad_v.astype(BF16)
+    yield 2.0
+    vec[of_q, :] = column_sum(gpacked[:, :D])
+    vec[of_v, :] = column_sum(gpacked[:, 2 * D:])
+    gn[...] = dot(gpacked[:, :D], tiles[0], NT) + dot(gpacked[:, D:2 * D], tiles[1], NT) + dot(gpacked[:, 2 * D:], tiles[2], NT)
     yield 1.5
-    need(("tiles", 0))
+    norm_backward(h, f.rows[gain:gain + 1, :], gn, g, vec, lines[0], lines[1])
+
+
+def chain_pieces(f, need, later, load, near_out, spans):
+    g, gn, gmix, vec, rows, gq, gkv, tiles = f.g, f.gn, f.gmix, f.vec, f.rows, f.gq, f.gkv, f.tiles
+    D = g.shape[1]
+    h = f.h.at[0]
+    yield 1.0
+    need(("g", 0), ("tiles", 0), ("packed", 1), ("logsum", 1), ("h", 2))
+    yield from self_back_pieces(f, need, 3, 13, h, (13, 15, 17, 18, 19))
+    for number in (2, 3, 4):
+        later(number)
+    load(2)
+    f.stage = 1
+    yield 2.0
+    need(("tiles", 1), ("slope", 0))
+    gb, gh, slope = f.gb.at[2], f.gh.at[0], f.slope.at[0]
+    gb[...] = g[...].astype(BF16)
+    vec[12:13, :] = column_sum(gb[...])
+    for j in range(4):
+        if j:
+            yield 2.0
+        if j == 2:
+            load(3)
+            need(("tiles", 2),)
+        cols, base = slice(j * D, (j + 1) * D), (4, 5, 0, 1)[j]
+        value = (dot(gb[...], tiles[base], NT) * slope[:, cols].astype(F32)).astype(BF16)
+        gh[:, cols] = value
+        f.vec_up[0:1, cols] = column_sum(value)
+        back = dot(value, tiles[base + 2], NT)
+        gn[...] = gn[...] + back if j else back
+    yield 1.5
+    load(4)
+    need(("h", 1),)
+    norm_backward(h, rows[2:3, :], gn, g, vec, 2, 5)
+    later(5)
+    f.stage = 2
+    yield 1.5
+    need(("tiles", 3), ("kv", 0), ("queries", 0), ("logsum", 2))
     gb = f.gb.at[1]
     gb[...] = g[...].astype(BF16)
     vec[11:12, :] = column_sum(gb[...])
-    gmix[...] = dot(gb[...], tiles[3], NT).astype(BF16)
+    gmix[...] = dot(gb[...], tiles[7], NT).astype(BF16)
     near, length = f.near_tokens.shape
     each = near // spans
     keys, size = each * length, g.shape[0] // spans
-    need(("kv", 0), ("queries", 0), ("logsum", 2), ("h", 0))
-    queries, kv, logsum = f.queries.at[0], f.kv.at[0], f.logsum.at[2]
+    queries, kv, logsum = f.queries.at[0], f.kv.at[0], f.logsum.at[0]
     for c in range(spans):
         yield 2.5
         srows, krows = slice(c * size, (c + 1) * size), slice(c * keys, (c + 1) * keys)
@@ -1298,42 +1290,24 @@
             gq[srows, a:a + 128] = of_q.astype(BF16)
             gkv[krows, a:a + 128], gkv[krows, b:b + 128] = of_k.astype(BF16), of_v.astype(BF16)
     yield 1.0
+    later(6)
     vec[9:10, :] = column_sum(gq[...])
     vec[10:11, :] = column_sum(gkv[:, D:])
-    gn[...] = dot(gq[...], tiles[0], NT)
+    gn[...] = dot(gq[...], tiles[4], NT)
     yield 1.5
-    norm_backward(f.h.at[0], rows[1:2, :], gn, g, vec, 1, 4)
-    f.stage = 1
+    need(("h", 0),)
+    norm_backward(h, rows[1:2, :], gn, g, vec, 1, 4)
+    f.stage = 3
     yield 1.0
-    gb = f.gb.at[0]
-    gb[...] = g[...].astype(BF16)
-    vec[8:9, :] = column_sum(gb[...])
-    gmix[...] = dot(gb[...], tiles[7], NT).astype(BF16)
-    need(("packed", 0), ("logsum", 0))
-    packed, logsum = f.packed.at[0], f.logsum.at[0]
-    for p in range(D // 128):
-        if p % 3 == 0:
-            yield 3.0
-        seen = f.allowed[...] != 0
-        seen = jnp.concatenate([seen, seen], axis=0)
-        a = p * 128
-        q, k, v = (slice(t * D + a, t * D + a + 128) for t in range(3))
-        of_q, of_k, of_v = attend_back(
-            packed[:, q], packed[:, k], packed[:, v], seen, logsum[:, p:p + 1], gmix[:, a:a + 128])
-        gpacked[:, q], gpacked[:, k], gpacked[:, v] = of_q.astype(BF16), of_k.astype(BF16), of_v.astype(BF16)
-    yield 2.0
-    vec[6:7, :] = column_sum(gpacked[:, :D])
-    vec[7:8, :] = column_sum(gpacked[:, 2 * D:])
-    gn[...] = dot(gpacked[:, :D], tiles[4], NT) + dot(gpacked[:, D:2 * D], tiles[5], NT) + dot(gpacked[:, 2 * D:], tiles[6], NT)
-    yield 1.5
-    norm_backward(f.tokens, rows[0:1, :], gn, g, vec, 0, 3)
-    f.stage = 2
+    need(("tiles", 4), ("packed", 0), ("logsum", 0))
+    yield from self_back_pieces(f, need, 0, 0, f.tokens, (0, 3, 6, 7, 8))
+    f.stage = 4
     for i in range(near // 2):
         yield 1.5
         krows = slice(2 * i * length, 2 * (i + 1) * length)
-        value = dot(gkv[krows, :D], tiles[1], NT) + dot(gkv[krows, D:], tiles[2], NT)
+        value = dot(gkv[krows, :D], tiles[5], NT) + dot(gkv[krows, D:], tiles[6], NT)
         near_out(i, value.reshape(2, length, D))
-    f.stage = 3
+    f.stage = 5
 
 
 def scatter_routes(parts, width):
@@ -1346,11 +1320,11 @@
 
 def scatter_kernel(dp_size, fsdp_size, chunks, count, plan, spans, *refs):
     factors = dict(zip(FACTORS, refs[:11]))
-    (first, near, near_tokens, rows, tokens, segments, g_in, vec_in, vec_up) = refs[11:20]
-    outs, grad_tokens, grad_near = refs[20:20 + count], refs[20 + count], refs[21 + count]
-    refs = refs[22 + count:]
+    (first, second, up, down, g_in, near, near_tokens, rows, tokens, segments, vec_in, vec_up_in) = refs[11:23]
+    outs, grad_tokens, grad_near = refs[23:23 + count], refs[23 + count], refs[24 + count]
+    refs = refs[25 + count:]
     f = types.SimpleNamespace(**dict(zip(FACTORS, refs[:11])))
-    (f.gq, f.gkv, f.tiles, f.gmix, f.gn, f.vec, f.allowed, small, near_stage), scratch = refs[11:20], refs[20:-5]
+    (f.gq, f.gkv, f.tiles, f.gmix, f.gn, f.vec, f.vec_up, f.gpacked, f.allowed, small, near_stage), scratch = refs[11:22], refs[22:-5]
     brought, loads, near_sem, send, recv = refs[-5:]
     f.near, f.near_tokens, f.rows, f.tokens, f.g, f.stage = near, near_tokens, rows, tokens, grad_tokens, 0
     D = tokens.shape[1]
@@ -1366,15 +1340,28 @@
         copy.start()
         arriving[name, index] = [copy]
 
-    def load(j):
-        copy = pltpu.make_async_copy(first.at[:, (j + 4) % 8 * D:((j + 4) % 8 + 1) * D], f.tiles.at[j], loads.at[j])
-        copy.start()
-        return copy
-    for number in range(4):
+    def load(number):
+        def across(array, col, slot):
+            return array.at[:, col * D:(col + 1) * D], f.tiles.at[slot]
+
+        def along(j, slot):
+            return down.at[j * D:(j + 1) * D, :], f.tiles.at[slot]
+        moves = (
+            [across(second, j, j) for j in range(4)], [along(0, 4), along(1, 5), across(up, 0, 6), across(up, 1, 7)],
+            [along(2, 0), along(3, 1), across(up, 2, 2), across(up, 3, 3)], [across(first, 4 + j, 4 + j) for j in range(4)],
+            [across(first, j, j) for j in range(4)])[number]
+        arriving["tiles", number] = [
+            pltpu.make_async_copy(src, dst, loads.at[4 * number + i]) for i, (src, dst) in enumerate(moves)]
+        for copy in arriving["tiles", number]:
+            copy.start()
+    for number in range(2):
         bring(number)
-    arriving["tiles", 0] = [load(j) for j in range(8)]
-    for number in range(4, len(ORDER)):
+    arriving["g", 0] = [pltpu.make_async_copy(g_in, grad_tokens, loads.at[20])]
+    arriving["g", 0][0].start()
+    load(0)
+    for number in range(2, len(ORDER)):
         bring(number)
+    load(1)
 
     def need(*wanted):
         for key in wanted:
@@ -1388,24 +1375,27 @@
         near_stage[...] = value
         near_copies.append(pltpu.make_async_copy(near_stage, grad_near.at[2 * i:2 * i + 2], near_sem))
         near_copies[-1].start()
-    chain = chain_pieces(f, need, near_out, spans)
+
+    def later(number):
+        bring(len(ORDER) + number)
+    chain = chain_pieces(f, need, later, load, near_out, spans)
 
     def require(stage):
         while f.stage < stage:
             next(chain)
-    makers = chunk_makers(f, need, lambda number: bring(len(ORDER) + number), require)
+    makers = chunk_makers(f, need, later, require)
     everything = pl.ds(0, place.size["y"])
     lead = tuple(place.size[name] for name in NAMES if name != "c")
 
     def pack():
-        require(2)
-        part, wide = outs[-1].shape[0], vec_up.shape[1]
+        require(4)
+        part, wide = outs[-1].shape[0], f.vec_up.shape[1]
         for index in itertools.product(*(range(place.size[name]) for name in NAMES)):
             i = ((index[0] * 2 + index[1]) * place.size["z"] + index[2]) * 2 + index[3]
             devices = dp_size * fsdp_size
             one, many = D // devices, wide // devices
             values = jnp.pad(f.vec[0:21, i * one:(i + 1) * one], ((0, 0), (0, 128 - one)))
-            ups = jnp.pad(vec_up[0:2, i * many:(i + 1) * many], ((0, 0), (0, 128 - many)))
+            ups = jnp.pad(f.vec_up[0:2, i * many:(i + 1) * many], ((0, 0), (0, 128 - many)))
             blank = jnp.zeros((part - 23, 128), F32)
             small[(*index, 0)] = jnp.concatenate([values, ups, blank], axis=0).astype(BF16)
 
@@ -1457,21 +1447,21 @@
         groups.append(members)
 
     fill_allowed(f.allowed, segments)
-    grad_tokens[...] = g_in[...]
     f.vec[...] = vec_in[...]
+    f.vec_up[...] = vec_up_in[...]
     greet(place)
 
     def chain_some(tick):
         left = CHAIN_SHARE
-        while f.stage < 3 and left > 0 and (f.stage != 1 or tick >= 5):
+        while f.stage < 5 and left > 0 and tick >= {1: 3, 3: 5}.get(f.stage, 0):
             left -= next(chain, 9.0)
     run_schedule(groups, SCATTER_STEPS, chain_some)
-    require(3)
+    require(5)
     sems.drain()
     near_copies.pop().wait()
 
 
-def scatter_all(mesh_shape, factors, first, near, near_tokens, rows, tokens, segment_ids, g, vec, vec_up, spans, owned, chunks,
+def scatter_all(mesh_shape, factors, weights, g, near, near_tokens, rows, tokens, segment_ids, vec, vec_up, spans, owned, chunks,
                 collective_id):
     dp_size, fsdp_size = mesh_shape
     size = {"y": dp_size // 2, "c": 2, "z": fsdp_size // 2, "x": 2}
@@ -1507,22 +1497,22 @@
             places.append((grad, landing, buffers))
         plan.append(places)
     vmem, hbm = pl.BlockSpec(memory_space=pltpu.VMEM), pl.BlockSpec(memory_space=pl.ANY)
-    slots = {"active": 1, "gh": 1, "gpacked": 1, "packed": 1, "h": 1}
+    slots = {"active": 1, "gh": 1, "packed": 1, "h": 1, "slope": 1, "n": 3, "mixed": 2, "logsum": 1}
     return pl.pallas_call(
         functools.partial(scatter_kernel, dp_size, fsdp_size, chunks, len(owned), plan, spans),
         out_shape=[jax.ShapeDtypeStruct(shape, F32) for shape in (*owned, (T, D), near.shape)],
-        in_specs=[hbm] * 12 + [vmem] * 8,
+        in_specs=[hbm] * 16 + [vmem] * 7,
         out_specs=[vmem] * (len(owned) + 1) + [hbm],
         scratch_shapes=[
             pltpu.VMEM((slots.get(name, factors[name].shape[0]),) + factors[name].shape[1:], factors[name].dtype)
             for name in FACTORS
         ] + [
             pltpu.VMEM((T, D), BF16), pltpu.VMEM((count_near * length, 2 * D), BF16), pltpu.VMEM((8, D, D), BF16),
-            pltpu.VMEM((T, D), BF16), pltpu.VMEM((T, D), F32), pltpu.VMEM((24, D), F32), pltpu.VMEM((T, T), jnp.int32),
-            pltpu.VMEM(whole + (1, 32, 128), BF16), pltpu.VMEM((2, length, D), F32),
+            pltpu.VMEM((T, D), BF16), pltpu.VMEM((T, D), F32), pltpu.VMEM((24, D), F32), pltpu.VMEM(vec_up.shape, F32),
+            pltpu.VMEM((T, 3 * D), BF16), pltpu.VMEM((T, T), jnp.int32), pltpu.VMEM(whole + (1, 32, 128), BF16), pltpu.VMEM((2, length, D), F32),
         ] + shapes + [
             pltpu.SemaphoreType.DMA((len(ORDER) + len(LATER),)),
-            pltpu.SemaphoreType.DMA((8,)),
+            pltpu.SemaphoreType.DMA((21,)),
             pltpu.SemaphoreType.DMA,
             pltpu.SemaphoreType.DMA((count,)),
             pltpu.SemaphoreType.DMA((count,)),
@@ -1530,8 +1520,7 @@
         compiler_params=pltpu.CompilerParams(
             collective_id=collective_id, has_side_effects=True, vmem_limit_bytes=VMEM_MOST),
         name="scatter_gradients",
-    )(*[factors[name] for name in FACTORS], first, near, near_tokens, rows, tokens, segment_ids,
-      g, vec, vec_up)
+    )(*[factors[name] for name in FACTORS], *weights, g, near, near_tokens, rows, tokens, segment_ids, vec, vec_up)
 
 
 PLACES = ((0, 0), (0, 3), (0, 4), (0, 5), (0, 7), (1, 0), (2, 0), (3, 0), (3, 3), (4, 0), (5, 0))
@@ -1572,11 +1561,11 @@
             mesh_shape, shards, tuple((w, c * D) for w, c in PLACES), vectors + ups, table, tokens, segment_ids,
             near, near_tokens, spans, 1)
         wholes = [w.reshape(-1, w.shape[-1]) for w in wholes]
-        (gradient, vec, vec_up), made = run_backward(cotangent, segment_ids, rows, h, saved, wholes[1:])
+        (gradient, vec, vec_up), made = run_backward(cotangent, rows, h, saved["slope"], *wholes[4:6])
         owned = [(w.shape[0] // devices, w.shape[1]) for w in wholes] + [(32, 128)]
         *owned, gradient, grad_neighbours = scatter_all(
-            mesh_shape, {**saved, **made, "h": h}, wholes[0], near, near_tokens, rows, tokens, segment_ids, gradient, vec, vec_up,
-            spans, owned, table[::-1], 2)
+            mesh_shape, {**saved, **made, "h": h}, (wholes[0], wholes[3], wholes[1], wholes[2]), gradient, near, near_tokens, rows,
+            tokens, segment_ids, vec, vec_up, spans, owned, table[::-1], 2)
     else:
         small = jnp.concatenate(vectors + [bias_up_one.reshape(-1, part), bias_up_two.reshape(-1, part)])
         small = jnp.pad(small, ((0, -small.shape[0] % 32), (0, -part % 128)))

time: 356 us -> 341 us (0.958)
  Pallas kernels: 348 us -> 333 us
    pallas_call x1, Pallas kernels: 24 us -> 11.4 us  [run_backward(): pl.pallas_call(backward_kernel, out_shape=[shape((T, D), F32), shape((24,...]
where the time goes in v2:
time: 341 us; the launch traced here: 338 us
  Pallas kernels  333 us (98%)
  local copies, waits for them, and re-layouts  3.5 us (1%)
    pallas_call x1, Pallas kernels, gather_and_run(): pl.pallas_call(functools.partial(forward_kernel, dp_size, fsdp_size, chun...  157 us
    pallas_call x1, Pallas kernels, scatter_all(): pl.pallas_call(functools.partial(scatter_kernel, dp_size, fsdp_size, chun...  155 us
    pallas_call x1, Pallas kernels, run_backward(): pl.pallas_call(backward_kernel, out_shape=[shape((T, D), F32), shape((24,...  11.4 us

profile of v2, /device:TPU:0, one launch (start us, length us, event | category | flops | bytes accessed | tf_op | source)
XLA Modules:
  0.0 338.0 jit_solution(13344691383183473077)
XLA Ops:
  0.7 0.8 copy.44
  1.4 0.1 reshape.75
  1.5 0.5 and_select_fusion.ids.refs_8_
  2.0 3.4 arrange_neighbours.1
  5.4 157.3 %gather_and_forward.1 = (bf16[2,2,4,2,24,6144]{5,4,3,2,1,0:T(8,128)(2,1)}, bf16[2,2,4,2,24,3072]{5,4,3,2,1,0:T(8,128)(2,1)}, bf16[2,2,4,2,96,768]{5,4,3,2,1,0:T(...) custom-call(bf16[24,2304]{1,0:T(8,128)(2,1)} %refs_0_.2, ...), custom_call_target="tpu_custom_call" | custom-call | tf_op jit(solution)/shard_map/gather_and_forward/pallas_call | solution.py:1025
  162.7 11.4 %backward.1 = (f32[256,768]{1,0:T(8,128)}, f32[24,768]{1,0:T(8,128)}, f32[8,3072]{1,0:T(8,128)}, bf16[5,256,768]{2,1,0:T(8,128)(2,1)}, bf16[2,256,3072]{2,1,0:T(8,128)(2,1)}) custom-call(bf16[256,768]{1,0:T(8,128)(2,1)} %refs_0_.3, f32[24,768]{1,0:T(8,128)} %get-tuple-element.77.refs_1_.refs_18_, f32[4,256,768]{2,1,0:T(8,128)} %get-tuple-element.78.refs_2_.refs_9_, ...), custom_call_target="tpu_custom_call" | custom-call | tf_op jit(solution)/shard_map/backward/pallas_call | solution.py:1095
  174.1 155.2 %scatter_gradients.1 = (f32[24,6144]{1,0:T(8,128)}, f32[24,3072]{1,0:T(8,128)}, f32[96,768]{1,0:T(8,128)}, f32[24,3072]{1,0:T(8,128)}, f32[24,3072]{1,0:T(8,128)...) custom-call(bf16[5,256,768]{2,1,0:T(8,128)(2,1)} %get-tuple-element.74.refs_0_, ...), custom_call_target="tpu_custom_call" | custom-call | tf_op jit(solution)/shard_map/scatter_gradients/pallas_call | solution.py:1501
  329.4 0.0 copy-start
  329.4 5.7 %split_gradients.1 = (f32[3,24]{1,0:T(4,128)}, f32[10,24]{1,0:T(8,128)}, f32[24,2304]{1,0:T(8,128)}, f32[24,768]{1,0:T(8,128)}, f32[24,768]{1,0:T(8,128)}, /*ind...) custom-call(f32[24,6144]{1,0:T(8,128)} %get-tuple-element.96.refs_0_, ...), custom_call_target="tpu_custom_call" | custom-call | tf_op jit(solution)/shard_map/split_gradients/pallas_call | solution.py:304
  335.1 1.8 copy.47
  336.9 0.0 copy-done
  336.9 0.9 copy.48
Async XLA Ops:
  329.4 7.5 %copy-start = (f32[256,768]{1,0:T(8,128)S(1)}, f32[256,768]{1,0:T(8,128)}, u32[]{:S(2)}) copy-start(f32[256,768]{1,0:T(8,128)} %get-tuple-element.143) | copy-start | bytes 2359300

commit v3 on v2

--- a/solution.py
+++ b/solution.py
@@ -14,10 +14,10 @@
 MESH = pl.DeviceIdType.MESH
 ROUTES = ((("z", "x", "y"), 1), (("z", "y", "x"), 1), (("x", "z", "y"), 2), (("y", "z", "x"), 2))
 NAMES = ("y", "c", "z", "x")
-GATHER_STEPS = (0, 1, 2, 3, 4, 6, 8)
+GATHER_STEPS = (0, 1, 2, 3, 4, 6, 7)
 VMEM_MOST = 63 * 2 ** 20
 COMPUTE_SHARE, CHAIN_SHARE = 3.5, 3.5
-SCATTER_STEPS = (0, 2, 4, 5, 6, 7, 8)
+SCATTER_STEPS = (0, 1, 3, 4, 5, 6, 7)
 LANDINGS, WINDOW = 6, 8
 
 
@@ -276,40 +276,46 @@
 
 
 def split_kernel(D, *refs):
-    one, up_one, down_one, two, up_two, down_two, small, near_in, ids = refs[:9]
+    one, up_one, down_one, two, up_two, down_two, small, out_in, tokens_in, near_in, ids = refs[:11]
     (gains_a, biases_a, qkv_a, out_a, cross_q, cross_kv, cross_out, g_up_a, bias_up_a, g_down_a,
-     gains_b, biases_b, qkv_b, out_b, g_up_b, bias_up_b, g_down_b, near, sems) = refs[9:]
-    copies = [pltpu.make_async_copy(near_in.at[j], near.at[ids[j]], sems.at[j]) for j in range(near.shape[0])]
-    for copy in copies:
+     gains_b, biases_b, qkv_b, out_b, g_up_b, bias_up_b, g_down_b, out, grad_tokens, near, stage, sems) = refs[11:]
+    count = near.shape[0]
+    arriving = [pltpu.make_async_copy(near_in.at[j], stage.at[j], sems.at[j]) for j in range(count)]
+    leaving = [pltpu.make_async_copy(stage.at[j], near.at[ids[j]], sems.at[count + j]) for j in range(count)]
+    for copy in arriving:
         copy.start()
     for src, dst in (
             (one[:, 0:3 * D], qkv_a), (one[:, 3 * D:4 * D], out_a), (one[:, 4 * D:5 * D], cross_q),
             (one[:, 5 * D:7 * D], cross_kv), (one[:, 7 * D:8 * D], cross_out), (up_one[...], g_up_a), (down_one[...], g_down_a),
-            (two[:, 0:3 * D], qkv_b), (two[:, 3 * D:4 * D], out_b), (up_two[...], g_up_b), (down_two[...], g_down_b)):
+            (two[:, 0:3 * D], qkv_b), (two[:, 3 * D:4 * D], out_b), (up_two[...], g_up_b), (down_two[...], g_down_b),
+            (out_in[...], out), (tokens_in[...], grad_tokens)):
         dst[...] = src
+    for came, goes in zip(arriving, leaving):
+        came.wait()
+        goes.start()
     start = 0
     for ref in (gains_a, biases_a, gains_b, biases_b, bias_up_a, bias_up_b):
         ref[...] = small[start:start + ref.shape[0], :ref.shape[1]]
         start += ref.shape[0]
-    for copy in copies:
+    for copy in leaving:
         copy.wait()
 
 
-def split_gradients(owned, near, near_index, D, quarter, part):
+def split_gradients(owned, out, grad_tokens, near, near_index, D, quarter, part):
     rows = owned[2].shape[0]
     shapes = [(3, part), (10, part), (part, 3 * D), (part, D), (part, D), (part, 2 * D), (part, D), (part, quarter * D),
               (1, quarter * part), (rows, D), (2, part), (6, part), (part, 3 * D), (part, D), (part, quarter * D),
-              (1, quarter * part), (rows, D), near.shape]
+              (1, quarter * part), (rows, D), out.shape, grad_tokens.shape, near.shape]
     vmem, hbm = pl.BlockSpec(memory_space=pltpu.VMEM), pl.BlockSpec(memory_space=pl.ANY)
     return pl.pallas_call(
         functools.partial(split_kernel, D),
-        out_shape=[jax.ShapeDtypeStruct(shape, jnp.float32) for shape in shapes],
-        in_specs=[vmem] * 8 + [pl.BlockSpec(memory_space=pltpu.SMEM)],
-        out_specs=[vmem] * 17 + [hbm],
-        scratch_shapes=[pltpu.SemaphoreType.DMA((near.shape[0],))],
+        out_shape=[jax.ShapeDtypeStruct(shape, BF16 if i == 17 else F32) for i, shape in enumerate(shapes)],
+        in_specs=[vmem] * 9 + [hbm, pl.BlockSpec(memory_space=pltpu.SMEM)],
+        out_specs=[vmem] * 19 + [hbm],
+        scratch_shapes=[pltpu.VMEM(near.shape, F32), pltpu.SemaphoreType.DMA((2 * near.shape[0],))],
         compiler_params=pltpu.CompilerParams(vmem_limit_bytes=VMEM_MOST),
         name="split_gradients",
-    )(*owned, near, near_index)
+    )(*owned, out, grad_tokens, near, near_index)
 
 
 F32, BF16 = jnp.float32, jnp.bfloat16
@@ -886,6 +892,16 @@
 
 
 def forward_pieces(e, h, tokens, first, up_a, down_a, second, up_b, down_b, small):
+    yield -len(SAVED) ** 2, 2.0
+    count = e.near.shape[0]
+    for j in range(count):
+        block, line = e.stored[0], e.stored_tokens[0:1, :]
+        for i in range(1, count):
+            chosen = e.chosen[j:j + 1, i:i + 1] != 0
+            block = jnp.where(jnp.broadcast_to(chosen, block.shape), e.stored[i], block)
+            line = jnp.where(chosen, e.stored_tokens[i:i + 1, :], line)
+        e.near[j], e.near_tokens[j:j + 1, :] = block, line
+    e.save("near", 0)
     yield 0, 1.5
     lines = [small[index] for index in itertools.product(*map(range, small.shape[:4]))]
     part = e.rows.shape[1] // len(lines)
@@ -907,17 +923,17 @@
     yield from ffn_pieces(e, 1, 4, h.at[3], up_b, down_b, 10, 14, (16, 20), finish)
 
 
-SAVED = ("n", "packed", "queries", "kv", "mixed", "logsum", "slope", "active")
+SAVED = ("n", "packed", "queries", "kv", "mixed", "logsum", "slope", "active", "near")
 
 
 def forward_kernel(dp_size, fsdp_size, chunks, places, count, spans, *refs):
     n = len(places)
-    shards, vectors, (tokens, segments, near, near_tokens) = refs[:n], refs[n:n + 6], refs[n + 6:n + 10]
-    refs = refs[n + 10:]
-    wholes, (out, h_out, rows), saved = refs[:count - 1], refs[count - 1:count + 2], dict(zip(SAVED, refs[count + 2:count + 10]))
-    refs = refs[count + 10:]
-    landing, held, (h, allowed, total, bias_up) = refs[:count], dict(zip(SAVED, refs[count:count + 8])), refs[count + 8:count + 12]
-    kept, saves, send, recv = refs[count + 12:]
+    shards, vectors, (tokens, segments, chosen, stored, stored_tokens) = refs[:n], refs[n:n + 6], refs[n + 6:n + 11]
+    refs = refs[n + 11:]
+    wholes, (out, h_out, rows, near_tokens), saved = refs[:count - 1], refs[count - 1:count + 3], dict(zip(SAVED, refs[count + 3:count + 12]))
+    refs = refs[count + 12:]
+    landing, held, (h, allowed, total, bias_up) = refs[:count], dict(zip(SAVED, refs[count:count + 9])), refs[count + 9:count + 13]
+    kept, saves, send, recv = refs[count + 13:]
     place = Place(dp_size, fsdp_size)
     here = tuple(place.at[name] for name in NAMES)
     for shard, (which, col) in zip(shards, places):
@@ -959,8 +975,8 @@
             pending.pop(name).wait()
 
     fill_allowed(allowed, segments)
-    e = types.SimpleNamespace(**held, rows=rows, bias_up=bias_up, allowed=allowed, near=near, near_tokens=near_tokens, spans=spans,
-             total=total, out=out, save=save, free=free)
+    e = types.SimpleNamespace(**held, rows=rows, bias_up=bias_up, allowed=allowed, near_tokens=near_tokens, spans=spans,
+             chosen=chosen, stored=stored, stored_tokens=stored_tokens, total=total, out=out, save=save, free=free)
     work = forward_pieces(e, h, tokens, *landing)
     ahead = next(work, None)
     groups, slot = [], 0
@@ -980,29 +996,7 @@
         copy.wait()
 
 
-def arrange_kernel(ids, neighbours, stored_tokens, near, near_tokens, sems):
-    copies = [pltpu.make_async_copy(neighbours.at[ids[j]], near.at[j], sems.at[j]) for j in range(near.shape[0])]
-    for copy in copies:
-        copy.start()
-    for j in range(near.shape[0]):
-        near_tokens[j:j + 1, :] = stored_tokens[pl.ds(ids[j], 1), :]
-    for copy in copies:
-        copy.wait()
-
-
-def arrange(near_index, neighbours, neighbour_tokens):
-    vmem, hbm = pl.BlockSpec(memory_space=pltpu.VMEM), pl.BlockSpec(memory_space=pl.ANY)
-    return pl.pallas_call(
-        arrange_kernel,
-        out_shape=[jax.ShapeDtypeStruct(x.shape, x.dtype) for x in (neighbours, neighbour_tokens)],
-        in_specs=[pl.BlockSpec(memory_space=pltpu.SMEM), hbm, vmem],
-        out_specs=[vmem, vmem],
-        scratch_shapes=[pltpu.SemaphoreType.DMA((neighbours.shape[0],))],
-        name="arrange_neighbours",
-    )(near_index, neighbours, neighbour_tokens)
-
-
-def gather_and_run(mesh_shape, shards, places, vectors, chunks, tokens, segment_ids, neighbours, neighbour_tokens,
+def gather_and_run(mesh_shape, shards, places, vectors, chunks, tokens, segment_ids, near_index, neighbours, neighbour_tokens,
                    spans, collective_id):
     dp_size, fsdp_size = mesh_shape
     size = {"y": dp_size // 2, "c": 2, "z": fsdp_size // 2, "x": 2}
@@ -1020,15 +1014,16 @@
     shape = jax.ShapeDtypeStruct
     held = {"n": ((T, D), BF16, 5), "packed": ((T, 3 * D), BF16, 2), "queries": ((T, D), BF16, 1),
             "kv": ((near * length, 2 * D), BF16, 1), "mixed": ((T, D), BF16, 3), "logsum": ((2 * T, 128), F32, 3),
-            "slope": ((T, FF), BF16, 2), "active": ((T, FF), BF16, 2)}
+            "slope": ((T, FF), BF16, 2), "active": ((T, FF), BF16, 2), "near": (neighbours.shape, BF16, 1)}
+    chosen = (near_index[:, None] == jnp.arange(near)[None, :]).astype(jnp.int32)
     n, vmem, hbm = len(shards), pl.BlockSpec(memory_space=pltpu.VMEM), pl.BlockSpec(memory_space=pl.ANY)
     results = pl.pallas_call(
         functools.partial(forward_kernel, dp_size, fsdp_size, chunks, places, len(shapes), spans),
         out_shape=[shape(lead + s, BF16) for s in shapes[:-1]]
-        + [shape((T, D), BF16), shape((4, T, D), F32), shape((24, D), F32)]
+        + [shape((T, D), BF16), shape((4, T, D), F32), shape((24, D), F32), shape((near, length), jnp.int32)]
         + [shape((times,) + s, kind) for s, kind, times in held.values()],
-        in_specs=[vmem] * (n + 10),
-        out_specs=[hbm] * (len(shapes) - 1) + [vmem, hbm, vmem] + [hbm] * 8,
+        in_specs=[vmem] * (n + 11),
+        out_specs=[hbm] * (len(shapes) - 1) + [vmem, hbm, vmem, vmem] + [hbm] * 9,
         scratch_shapes=[pltpu.VMEM(lead + s, BF16) for s in shapes]
         + [pltpu.VMEM(s, kind) for s, kind, _ in held.values()]
         + [pltpu.VMEM((4, T, D), F32), pltpu.VMEM((T, T), jnp.int32), pltpu.VMEM((T, D), F32), pltpu.VMEM((2, FF), F32)]
@@ -1041,8 +1036,8 @@
         compiler_params=pltpu.CompilerParams(
             collective_id=collective_id, has_side_effects=True, vmem_limit_bytes=63 * 2 ** 20),
         name="gather_and_forward",
-    )(*shards, *vectors, tokens, segment_ids, neighbours, neighbour_tokens)
-    return results[:len(shapes) - 1], results[len(shapes) - 1:len(shapes) + 2], dict(zip(SAVED, results[len(shapes) + 2:]))
+    )(*shards, *vectors, tokens, segment_ids, chosen, neighbours, neighbour_tokens)
+    return results[:len(shapes) - 1], results[len(shapes) - 1:len(shapes) + 3], dict(zip(SAVED, results[len(shapes) + 3:]))
 
 
 def ffn_chain(e, i, h_in, w_up, w_down, gain, norm, rows):
@@ -1556,15 +1551,15 @@
     near_index = neighbour_ids.reshape(-1) % store_count
     if kernels:
         ups = [bias_up_one.reshape(1, -1), bias_up_two.reshape(1, -1)]
-        near, near_tokens = arrange(near_index, neighbours, neighbour_tokens)
-        wholes, (out, h, rows), saved = gather_and_run(
+        wholes, (out, h, rows, near_tokens), saved = gather_and_run(
             mesh_shape, shards, tuple((w, c * D) for w, c in PLACES), vectors + ups, table, tokens, segment_ids,
-            near, near_tokens, spans, 1)
+            near_index, neighbours, neighbour_tokens, spans, 1)
         wholes = [w.reshape(-1, w.shape[-1]) for w in wholes]
         (gradient, vec, vec_up), made = run_backward(cotangent, rows, h, saved["slope"], *wholes[4:6])
         owned = [(w.shape[0] // devices, w.shape[1]) for w in wholes] + [(32, 128)]
         *owned, gradient, grad_neighbours = scatter_all(
-            mesh_shape, {**saved, **made, "h": h}, (wholes[0], wholes[3], wholes[1], wholes[2]), gradient, near, near_tokens, rows,
+            mesh_shape, {**saved, **made, "h": h}, (wholes[0], wholes[3], wholes[1], wholes[2]), gradient,
+            saved["near"].reshape(neighbours.shape), near_tokens, rows,
             tokens, segment_ids, vec, vec_up, spans, owned, table[::-1], 2)
     else:
         small = jnp.concatenate(vectors + [bias_up_one.reshape(-1, part), bias_up_two.reshape(-1, part)])
@@ -1588,7 +1583,8 @@
         grads.append(vectors.reshape(-1, 128).astype(BF16))
         owned = [lax.psum_scatter(g.astype(F32), ("dp", "fsdp"), scatter_dimension=0, tiled=True) for g in grads]
         grad_neighbours = jnp.take(grad_neighbours, near_index, axis=0)
-    *split, grad_neighbours = split_gradients(owned, grad_neighbours, near_index, D, quarter, part)
+    *split, out, gradient, grad_neighbours = split_gradients(
+        owned, out, gradient, grad_neighbours, near_index, D, quarter, part)
     split[8], split[15] = split[8].reshape(-1), split[15].reshape(-1)
     return (out, gradient, grad_neighbours, *split)
 

time: 341 us -> 336 us (0.985)
  no operation moved by 1% of the time
where the time goes in v3:
time: 336 us; the launch traced here: 333 us
  Pallas kernels  331 us (99%)
    pallas_call x1, Pallas kernels, gather_and_run(): pl.pallas_call(functools.partial(forward_kernel, dp_size, fsdp_size, chun...  160 us
    pallas_call x1, Pallas kernels, scatter_all(): pl.pallas_call(functools.partial(scatter_kernel, dp_size, fsdp_size, chun...  153 us
    pallas_call x1, Pallas kernels, run_backward(): pl.pallas_call(backward_kernel, out_shape=[shape((T, D), F32), shape((24,...  11.5 us

profile of v3, /device:TPU:0, one launch (start us, length us, event | category | flops | bytes accessed | tf_op | source)
XLA Modules:
  0.0 333.1 jit_solution(13903355344583388057)
XLA Ops:
  0.7 0.8 copy.44
  1.4 0.1 reshape.99
  1.5 0.0 copy-start
  1.5 0.7 fusion.refs_19_
  2.2 159.7 %gather_and_forward.1 = (bf16[2,2,4,2,24,6144]{5,4,3,2,1,0:T(8,128)(2,1)}, bf16[2,2,4,2,24,3072]{5,4,3,2,1,0:T(8,128)(2,1)}, bf16[2,2,4,2,96,768]{5,4,3,2,1,0:T(...) custom-call(bf16[24,2304]{1,0:T(8,128)(2,1)} %refs_0_.2, ...), custom_call_target="tpu_custom_call" | custom-call | tf_op jit(solution)/shard_map/gather_and_forward/pallas_call | solution.py:1020
  161.9 11.5 %backward.1 = (f32[256,768]{1,0:T(8,128)}, f32[24,768]{1,0:T(8,128)}, f32[8,3072]{1,0:T(8,128)}, bf16[5,256,768]{2,1,0:T(8,128)(2,1)}, bf16[2,256,3072]{2,1,0:T(8,128)(2,1)}) custom-call(bf16[256,768]{1,0:T(8,128)(2,1)} %refs_0_.3, f32[24,768]{1,0:T(8,128)} %get-tuple-element.76.refs_1_.refs_18_, f32[4,256,768]{2,1,0:T(8,128)} %get-tuple-element.77.refs_2_.refs_9_, ...), custom_call_target="tpu_custom_call" | custom-call | tf_op jit(solution)/shard_map/backward/pallas_call | solution.py:1090
  173.4 0.0 copy-done
  173.4 153.0 %scatter_gradients.1 = (f32[24,6144]{1,0:T(8,128)}, f32[24,3072]{1,0:T(8,128)}, f32[96,768]{1,0:T(8,128)}, f32[24,3072]{1,0:T(8,128)}, f32[24,3072]{1,0:T(8,128)...) custom-call(bf16[5,256,768]{2,1,0:T(8,128)(2,1)} %get-tuple-element.73.refs_0_, ...), custom_call_target="tpu_custom_call" | custom-call | tf_op jit(solution)/shard_map/scatter_gradients/pallas_call | solution.py:1496
  326.4 6.5 %split_gradients.1 = (f32[3,24]{1,0:T(4,128)}, f32[10,24]{1,0:T(8,128)}, f32[24,2304]{1,0:T(8,128)}, f32[24,768]{1,0:T(8,128)}, f32[24,768]{1,0:T(8,128)}, /*ind...) custom-call(f32[24,6144]{1,0:T(8,128)} %get-tuple-element.96.refs_0_, ...), custom_call_target="tpu_custom_call" | custom-call | tf_op jit(solution)/shard_map/split_gradients/pallas_call | solution.py:310
  (1 shorter events, 0.0 us)
Async XLA Ops:
  1.5 171.9 %copy-start = (s32[8]{0:T(128)}, s32[8]{0:T(128)S(1)}, u32[]{:S(2)}) copy-start(s32[8]{0:T(128)S(1)} %and_select_fusion.refs_10_) | copy-start | bytes 100
